TPU v7x, 32 devices: a whole 2x2x4 slice. The times are simulated.
32 devices in a mesh: seq: 4 (over y, x), fsdp: 8 (over z, core).
Axes of the slice: x: 2, y: 2, z: 4, core: 2. Of those that a mesh axis runs over, the one named last changes fastest.
Arguments:
- hidden: bfloat16 [8, 1024, 1024], P('fsdp', 'seq'), may hold values from -6 to 6
- lengths: int32 [8], P('fsdp'), may hold values from 1 to 1024, 5120 in all
- expert_ids: int32 [8, 1024, 1], P('fsdp', 'seq'), may hold values from 0 to 15; in each aligned block of 256 rows (0 to 255, 256 to 511, ..., all dimensions but the last counted through in order) at most 32 rows name the same one
- attn_gain: bfloat16 [1024], P(('seq', 'fsdp')), may hold values from 0.5 to 1.5
- qkv_weight: bfloat16 [1024, 3072], P(('seq', 'fsdp')), may hold values from -0.1875 to 0.1875
- out_weight: bfloat16 [1024, 1024], P(('seq', 'fsdp')), may hold values from -2 to 2
- moe_gain: bfloat16 [1024], P(('seq', 'fsdp')), may hold values from 0.5 to 1.5
- router_weight: bfloat16 [1024, 16], P(('seq', 'fsdp')), may hold values from -0.09375 to 0.09375
- expert_in: bfloat16 [16, 1024, 4096], P('fsdp', None, 'seq'), may hold values from -0.1875 to 0.1875
- expert_out: bfloat16 [16, 4096, 1024], P('fsdp', 'seq'), may hold values from -12 to 12
- out_grad: bfloat16 [8, 1024, 1024], P('fsdp', 'seq'), may hold values from -6 to 6
Outputs:
- output: bfloat16 [8, 1024, 1024], P('fsdp', 'seq')
- input_grad: float32 [8, 1024, 1024], P('fsdp', 'seq')
- attn_gain_grad: float32 [1024], P(('seq', 'fsdp'))
- qkv_grad: float32 [1024, 3072], P(('seq', 'fsdp'))
- out_weight_grad: float32 [1024, 1024], P(('seq', 'fsdp'))
- moe_gain_grad: float32 [1024], P(('seq', 'fsdp'))
- router_grad: float32 [1024, 16], P(('seq', 'fsdp'))
- expert_in_grad: float32 [16, 1024, 4096], P('fsdp', None, 'seq')
- expert_out_grad: float32 [16, 4096, 1024], P('fsdp', 'seq')
Inputs may be any that keep to these rules, and one draw needn't show every extreme that they name: `lengths`: the longest slot holds exactly 1024 valid positions. `expert_ids`: in each aligned block of 256 tokens (the tokens of one device, slots first, then positions), no expert is named more than 32 times, and in some block one expert is named exactly 32 times.
All inputs are finite; a program needn't handle non-finite values. No bound on the sum of `lengths` on one device may be relied on, other than what follows from the above.
Results may differ from a plain program's by a relative error of at most 0.017.
Values may be sent and summed in bfloat16 or wider, within the bound.
A program may use at most 192 MiB of HBM per device.

v0:
```python
import jax
import jax.numpy as jnp
from jax import lax
from jax.sharding import PartitionSpec as P

HEAD_DIM = 64
QBLOCK = 512


EPS = 1e-05
MASKED = -1e30


def scaled_norm(value, gain):
    return value * lax.rsqrt(jnp.mean(value * value, axis=-1, keepdims=True) + EPS) * gain


def gelu_tanh(value):
    return jax.nn.gelu(value, approximate=True)


def times_transposed(left, right):
    return lax.dot_general(
        left, right, (((1,), (1,)), ((), ())), preferred_element_type=jnp.float32
    )


def transposed_times(left, right):
    return lax.dot_general(
        left, right, (((0,), (0,)), ((), ())), preferred_element_type=jnp.float32
    )


def to_heads(value):
    return lax.all_to_all(value, "seq", split_axis=2, concat_axis=0, tiled=True)


def to_tokens(value):
    return lax.all_to_all(value, "seq", split_axis=0, concat_axis=2, tiled=True)


def to_owners(value):
    return lax.all_to_all(value, "fsdp", split_axis=0, concat_axis=0, tiled=True)


def to_sources(value):
    return lax.all_to_all(value, "fsdp", split_axis=0, concat_axis=0, tiled=True)


def spread_rows(value):
    return lax.all_gather(value, "seq", axis=2, tiled=True)


def collect_rows(value):
    return lax.psum_scatter(value, "seq", scatter_dimension=2, tiled=True)


def masked_scores(block_query, keys, start, length, scale):
    scores = (
        jnp.einsum("qhd,khd->hqk", block_query, keys, preferred_element_type=jnp.float32) * scale
    )
    rows = start + jnp.arange(block_query.shape[0], dtype=jnp.int32)
    columns = jnp.arange(keys.shape[0], dtype=jnp.int32)
    keep = (columns[None, :] <= rows[:, None]) & (columns[None, :] < length)
    return jnp.where(keep[None], scores, MASKED)


def shards(
    hidden,
    lengths,
    expert_ids,
    attn_gain,
    qkv_weight,
    out_weight,
    moe_gain,
    router_weight,
    expert_in,
    expert_out,
    out_grad,
):
    seq_count = lax.axis_size("seq")
    seq_place = lax.axis_index("seq")
    tokens = hidden.shape[1]
    width = hidden.shape[2]
    full_len = tokens * seq_count
    gain_one, weight_qkv, weight_mix, gain_two, weight_route = (
        lax.all_gather(attn_gain, ("seq", "fsdp"), axis=0, tiled=True),
        lax.all_gather(qkv_weight, ("seq", "fsdp"), axis=0, tiled=True),
        lax.all_gather(out_weight, ("seq", "fsdp"), axis=0, tiled=True),
        lax.all_gather(moe_gain, ("seq", "fsdp"), axis=0, tiled=True),
        lax.all_gather(router_weight, ("seq", "fsdp"), axis=0, tiled=True),
    )
    experts_all = weight_route.shape[1]
    expert_local = expert_in.shape[0]
    owners = experts_all // expert_local
    capacity = max(2, 2 * tokens // experts_all)
    heads_local = width // seq_count // HEAD_DIM
    group_width = width // seq_count
    scale = HEAD_DIM ** (-0.5)
    length = lengths[0]
    position = seq_place * tokens + jnp.arange(tokens, dtype=jnp.int32)
    valid = (position < length).astype(jnp.float32)[:, None]
    inputs = hidden[0].astype(jnp.float32)
    normed, norm_back = jax.vjp(scaled_norm, inputs, gain_one.astype(jnp.float32))
    normed = normed.astype(jnp.bfloat16)
    projected = jnp.dot(normed, weight_qkv, preferred_element_type=jnp.float32).astype(jnp.bfloat16)
    grouped = to_heads(projected.reshape(tokens, 3, width))
    query = grouped[:, 0].reshape(full_len, heads_local, HEAD_DIM)
    keys = grouped[:, 1].reshape(full_len, heads_local, HEAD_DIM)
    values = grouped[:, 2].reshape(full_len, heads_local, HEAD_DIM)
    starts = list(range(0, full_len, QBLOCK))
    outputs = []
    totals = []
    for start in starts:
        reach = full_len
        block_query = query[start : start + QBLOCK]
        scores = masked_scores(block_query, keys, start, length, scale)
        top = jnp.max(scores, axis=-1, keepdims=True)
        total = top + jnp.log(jnp.sum(jnp.exp(scores - top), axis=-1, keepdims=True))
        probs = jnp.exp(scores - total).astype(jnp.bfloat16)
        block_out = jnp.einsum("hqk,khd->qhd", probs, values, preferred_element_type=jnp.float32)
        outputs.append(block_out.astype(jnp.bfloat16))
        totals.append(total)
    attended = jnp.concatenate(outputs, axis=0).reshape(full_len, 1, group_width)
    mixed = to_tokens(attended).reshape(tokens, width)
    middle = inputs + jnp.dot(mixed, weight_mix, preferred_element_type=jnp.float32)
    normed_two, norm_two_back = jax.vjp(scaled_norm, middle, gain_two.astype(jnp.float32))
    normed_two = normed_two.astype(jnp.bfloat16)
    logits = jnp.dot(normed_two, weight_route, preferred_element_type=jnp.float32)
    chosen = expert_ids[0, :, 0]
    choose = chosen[:, None] == jnp.arange(experts_all, dtype=jnp.int32)[None, :]

    def gate_of(logit_rows):
        return jnp.sum(jnp.where(choose, jax.nn.softmax(logit_rows, axis=-1), 0.0), axis=-1)

    gate, gate_back = jax.vjp(gate_of, logits)
    counts = choose.astype(jnp.int32)
    ranks = jnp.sum(jnp.cumsum(counts, axis=0) * counts, axis=1) - 1
    slot = chosen * capacity + ranks
    dispatch = (
        jnp.arange(experts_all * capacity, dtype=jnp.int32)[:, None] == slot[None, :]
    ).astype(jnp.bfloat16)
    sent = jnp.dot(dispatch, normed_two, preferred_element_type=jnp.float32).astype(jnp.bfloat16)
    arrived = to_owners(sent.reshape(owners, expert_local, capacity, width))
    rows_all = spread_rows(arrived)
    weight_in, weight_out = (expert_in, expert_out)
    inner = jnp.einsum("sjcd,jdf->sjcf", rows_all, weight_in, preferred_element_type=jnp.float32)
    active, active_back = jax.vjp(gelu_tanh, inner)
    active = active.astype(jnp.bfloat16)
    partial_out = jnp.einsum(
        "sjcf,jfd->sjcd", active, weight_out, preferred_element_type=jnp.float32
    )
    produced = collect_rows(partial_out)
    returned = to_sources(produced.astype(jnp.bfloat16)).reshape(experts_all * capacity, width)
    back_rows = jnp.einsum("st,sd->td", dispatch, returned, preferred_element_type=jnp.float32)
    output = valid * (middle + gate[:, None] * back_rows)
    upstream = out_grad[0].astype(jnp.float32) * valid
    grad_returned = (upstream * gate[:, None]).astype(jnp.bfloat16)
    grad_gate = jnp.sum(upstream * back_rows, axis=1)
    grad_logits = gate_back(grad_gate)[0].astype(jnp.bfloat16)
    grad_route = transposed_times(normed_two, grad_logits)
    grad_normed_two = times_transposed(grad_logits, weight_route)
    grad_sent = jnp.dot(dispatch, grad_returned, preferred_element_type=jnp.float32).astype(
        jnp.bfloat16
    )
    grad_arrived = to_owners(grad_sent.reshape(owners, expert_local, capacity, width))
    grad_rows = spread_rows(grad_arrived)
    grad_active = jnp.einsum(
        "sjcd,jfd->sjcf", grad_rows, weight_out, preferred_element_type=jnp.float32
    )
    grad_weight_out = jnp.einsum(
        "sjcf,sjcd->jfd", active, grad_rows, preferred_element_type=jnp.float32
    )
    grad_inner = active_back(grad_active)[0].astype(jnp.bfloat16)
    grad_weight_in = jnp.einsum(
        "sjcd,sjcf->jdf", rows_all, grad_inner, preferred_element_type=jnp.float32
    )
    grad_rows_in = jnp.einsum(
        "sjcf,jdf->sjcd", grad_inner, weight_in, preferred_element_type=jnp.float32
    )
    grad_input_rows = collect_rows(grad_rows_in)
    expert_in_grad, expert_out_grad = (grad_weight_in, grad_weight_out)
    grad_back_rows = to_sources(grad_input_rows.astype(jnp.bfloat16)).reshape(
        experts_all * capacity, width
    )
    grad_normed_two = grad_normed_two + jnp.einsum(
        "st,sd->td", dispatch, grad_back_rows, preferred_element_type=jnp.float32
    )
    grad_middle, grad_gain_two = norm_two_back(grad_normed_two)
    grad_middle = grad_middle + upstream
    grad_attn = grad_middle.astype(jnp.bfloat16)
    grad_mix = transposed_times(mixed, grad_attn)
    grad_mixed = times_transposed(grad_attn, weight_mix).astype(jnp.bfloat16)
    grad_heads = to_heads(grad_mixed.reshape(tokens, 1, width)).reshape(
        full_len, heads_local, HEAD_DIM
    )
    grad_query = []
    grad_keys = jnp.zeros((full_len, heads_local, HEAD_DIM), jnp.float32)
    grad_values = jnp.zeros((full_len, heads_local, HEAD_DIM), jnp.float32)
    for number, start in enumerate(starts):
        reach = full_len
        block_query = query[start : start + QBLOCK]
        scores = masked_scores(block_query, keys, start, length, scale)
        probs = jnp.exp(scores - totals[number])
        probs_low = probs.astype(jnp.bfloat16)
        grad_out = grad_heads[start : start + QBLOCK]
        grad_values = grad_values.at[:reach].add(
            jnp.einsum("hqk,qhd->khd", probs_low, grad_out, preferred_element_type=jnp.float32)
        )
        grad_probs = jnp.einsum(
            "qhd,khd->hqk", grad_out, values, preferred_element_type=jnp.float32
        )
        grad_scores = (
            probs * (grad_probs - jnp.sum(grad_probs * probs, axis=-1, keepdims=True))
        ).astype(jnp.bfloat16)
        grad_query.append(
            jnp.einsum("hqk,khd->qhd", grad_scores, keys, preferred_element_type=jnp.float32)
            * scale
        )
        grad_keys = grad_keys.at[:reach].add(
            jnp.einsum("hqk,qhd->khd", grad_scores, block_query, preferred_element_type=jnp.float32)
            * scale
        )
    grad_grouped = jnp.stack([jnp.concatenate(grad_query, axis=0), grad_keys, grad_values], axis=1)
    grad_grouped = grad_grouped.astype(jnp.bfloat16).reshape(full_len, 3, group_width)
    grad_projected = to_tokens(grad_grouped).reshape(tokens, 3 * width)
    grad_qkv_weight = transposed_times(normed, grad_projected)
    grad_normed = times_transposed(grad_projected, weight_qkv)
    grad_inputs, grad_gain_one = norm_back(grad_normed)
    grad_inputs = grad_inputs + grad_middle
    gain_one_grad, qkv_weight_grad, mix_grad, gain_two_grad, route_grad = (
        lax.psum_scatter(grad_gain_one, ("seq", "fsdp"), scatter_dimension=0, tiled=True),
        lax.psum_scatter(grad_qkv_weight, ("seq", "fsdp"), scatter_dimension=0, tiled=True),
        lax.psum_scatter(grad_mix, ("seq", "fsdp"), scatter_dimension=0, tiled=True),
        lax.psum_scatter(grad_gain_two, ("seq", "fsdp"), scatter_dimension=0, tiled=True),
        lax.psum_scatter(grad_route, ("seq", "fsdp"), scatter_dimension=0, tiled=True),
    )
    return (
        output.astype(jnp.bfloat16)[None],
        grad_inputs[None],
        gain_one_grad,
        qkv_weight_grad,
        mix_grad,
        gain_two_grad,
        route_grad,
        expert_in_grad,
        expert_out_grad,
    )


def solution(mesh):
    placed = (
        P("fsdp", "seq", None),
        P("fsdp"),
        P("fsdp", "seq", None),
        P(("seq", "fsdp")),
        P(("seq", "fsdp"), None),
        P(("seq", "fsdp"), None),
        P(("seq", "fsdp")),
        P(("seq", "fsdp"), None),
        P("fsdp", None, "seq"),
        P("fsdp", "seq", None),
        P("fsdp", "seq", None),
    )
    return jax.shard_map(
        shards,
        mesh=mesh,
        in_specs=placed,
        out_specs=(
            P("fsdp", "seq", None),
            P("fsdp", "seq", None),
            P(("seq", "fsdp")),
            P(("seq", "fsdp"), None),
            P(("seq", "fsdp"), None),
            P(("seq", "fsdp")),
            P(("seq", "fsdp"), None),
            P("fsdp", None, "seq"),
            P("fsdp", "seq", None),
        ),
        check_vma=False,
    )
```

profile of v0, /device:TPU:0, one launch (start us, length us, event | category | flops | bytes accessed | tf_op | source)
XLA Modules:
  0.0 1116.4 jit_solution(15297391344962001983)
XLA Ops:
  9.6 43.1 %all-reduce.5 = (bf16[1024]{0:T(1024)(128)(2,1)S(1)}, bf16[1024]{0:T(1024)(128)(2,1)S(1)}) all-reduce(bf16[1024]{0:T(1024)(128)(2,1)S(1)} %dynamic-update-slice.8, bf16[1024]{0:T(1024)(128)(2,1)S(1)} %dynamic-update-slice.9), channel_id=1, replica_groups=mesh['seq'=4,'fsdp'=8] {'seq','fsdp'}, use_global_device_ids=true, to_apply=%add | all-reduce | flops 2048 | bytes 8192
  53.9 29.5 %all-gather.6.cloned.1.call-done = bf16[1024,3072]{1,0:T(8,128)(2,1)} async-done(((bf16[32,3072]{1,0:T(8,128)(2,1)}), bf16[1024,3072]{1,0:T(8,128)(2,1)}) %all-gather.6.cloned.1.call-update) | async-done | bytes 6291472 | tf_op jit(solution)/shard_map/all_gather | solution.py:88
  83.4 4.8 convolution_convert_fusion
  89.0 2.7 copy.83
  91.7 3.6 all-to-all-start
  97.9 23.4 %all-to-all-done = bf16[256,3,1024]{0,1,2:T(4,128)(2,1)S(1)} async-done(((bf16[256,3,1024]{0,1,2:T(4,128)(2,1)}), bf16[256,3,1024]{0,1,2:T(4,128)(2,1)S(1)}, u32[]{:S(2)}, u32[]{:S(2)}) %all-to-all-start) | async-done | bytes 1572896 | tf_op jit(solution)/shard_map/all_to_all | solution.py:35
  131.7 2.4 exponential_reduce_fusion
  135.8 2.4 exponential_reduce_fusion.1
  138.3 2.4 fusion.43
  140.7 2.4 fusion.42
  145.8 3.5 all-to-all-start.1
  150.0 10.3 all-to-all-done.1
  162.9 5.3 all-gather.8.cloned.1.call-done
  168.2 2.4 multiply_reduce_fusion.4
  171.3 29.9 %all_to_all.83 = bf16[8,2,32,1024]{3,2,1,0:T(8,128)(2,1)S(1)} all-to-all(bf16[8,2,32,1024]{3,2,1,0:T(8,128)(2,1)S(1)} %bitcast.238), channel_id=1, replica_groups=mesh['seq'=4,'fsdp'=8] {'fsdp'}, dimensions={0} | all-to-all | bytes 2097152 | tf_op jit(solution)/shard_map/all_to_all | solution.py:43
  202.4 49.8 %all-gather.10.cloned.1.call-done = bf16[8,2,128,1024]{3,2,0,1:T(8,128)(2,1)} async-done(((bf16[8,2,32,1024]{3,2,0,1:T(8,128)(2,1)}), bf16[8,2,128,1024]{3,2,0,1:T(8,128)(2,1)}) %all-gather.10.cloned.1.call-update) | async-done | bytes 4194320 | tf_op jit(solution)/shard_map/all_gather | solution.py:51
  252.2 7.7 fusion.17
  259.9 3.2 copy-done.38
  263.1 7.3 fusion.22
  270.5 86.6 %reduce-scatter.8.cloned.1.call-done = f32[8,2,32,1024]{3,2,0,1:T(8,128)} async-done(((f32[8,2,128,1024]{3,2,0,1:T(8,128)}), f32[8,2,32,1024]{3,2,0,1:T(8,128)}) %reduce-scatter.8.cloned.1.call-update) | async-done | bytes 2097168 | tf_op jit(solution)/shard_map/reduce_scatter | solution.py:55
  357.0 1.7 convert_element_type.126
  359.9 4.6 all-to-all-start.3
  364.5 56.3 %all-gather = bf16[32,32,16]{1,2,0:T(8,128)(2,1)S(1)} all-gather(bf16[1,32,16]{1,2,0:T(8,128)(2,1)S(1)} %bitcast.256), channel_id=1, replica_groups=mesh['seq'=4,'fsdp'=8] {'seq','fsdp'}, dimensions={0}, use_global_device_ids=true | all-gather | bytes 33792 | tf_op jit(solution)/shard_map/all_gather | solution.py:91
  422.7 2.7 fusion.57
  427.4 29.0 %all_to_all.84 = bf16[8,2,32,1024]{3,2,1,0:T(8,128)(2,1)S(1)} all-to-all(bf16[8,2,32,1024]{3,2,1,0:T(8,128)(2,1)S(1)} %bitcast.248), channel_id=1, replica_groups=mesh['seq'=4,'fsdp'=8] {'fsdp'}, dimensions={0} | all-to-all | bytes 2097152 | tf_op jit(solution)/shard_map/all_to_all | solution.py:43
  458.1 50.1 %all-gather.12.cloned.1.call-done = bf16[8,2,128,1024]{3,2,0,1:T(8,128)(2,1)} async-done(((bf16[8,2,32,1024]{3,2,0,1:T(8,128)(2,1)}), bf16[8,2,128,1024]{3,2,0,1:T(8,128)(2,1)}) %all-gather.12.cloned.1.call-update) | async-done | bytes 4194320 | tf_op jit(solution)/shard_map/all_gather | solution.py:51
  508.2 13.4 %fusion.6 = bf16[8,2,128,1024]{3,2,0,1:T(8,128)(2,1)S(1)} fusion(f32[2,8,128,1024]{3,2,1,0:T(8,128)} %copy-done.38, bf16[8,2,128,1024]{3,2,0,1:T(8,128)(2,1)} %all-gather.12.cloned.1.call-done, bf16[2,1024,1024]{2,1,0:T(8,128)(2,1)} %param.36), kind=kOutput, calls=%fused_computation.8 | convolution fusion | flops 4336910336 | bytes 20971520 | tf_op jit(solution)/shard_map/sjcd,jfd->sjcf/dot_general | solution.py:168
  521.6 2.1 copy-done.39
  523.7 6.8 fusion.25
  530.5 86.5 %reduce-scatter.10.cloned.1.call-done = f32[8,2,32,1024]{3,2,0,1:T(8,128)} async-done(((f32[8,2,128,1024]{3,2,0,1:T(8,128)}), f32[8,2,32,1024]{3,2,0,1:T(8,128)}) %reduce-scatter.10.cloned.1.call-update) | async-done | bytes 2097168 | tf_op jit(solution)/shard_map/reduce_scatter | solution.py:55
  617.1 1.7 convert_element_type.134
  619.9 4.8 all-to-all-start.5
  625.1 26.3 %all-to-all-done.5 = bf16[8,2,32,1024]{3,2,1,0:T(8,128)(2,1)} async-done(((bf16[8,2,32,1024]{3,2,1,0:T(8,128)(2,1)}), bf16[8,2,32,1024]{3,2,1,0:T(8,128)(2,1)}, u32[]{:S(2)}, u32[]{:S(2)}) %all-to-all-start.5) | async-done | bytes 1048608 | tf_op jit(solution)/shard_map/all_to_all | solution.py:47
  651.4 2.1 multiply_reduce_fusion.2
  653.4 2.7 fusion.52
  657.7 2.4 copy.98
  660.1 4.6 reduce.11
  664.7 2.0 reshape.436
  666.7 4.1 all-to-all-start.6
  670.9 2.2 fusion.91
  673.1 3.7 fusion.73
  677.1 1.9 all-to-all-done.6
  679.0 2.2 reshape.437
  682.3 4.8 fusion.97
  687.1 5.7 fusion.36
  692.8 3.6 copy.103
  696.4 7.8 multiply_reduce_fusion
  704.2 7.7 multiply_reduce_fusion.1
  712.4 8.4 multiply_convert_fusion
  720.8 2.0 copy-done.2
  725.7 2.0 copy.101
  727.7 3.2 fusion.106
  732.0 2.0 copy.102
  734.0 4.9 pad_maximum_fusion
  738.9 27.6 %all_to_all.85 = bf16[1024,3,256]{2,1,0:T(4,128)(2,1)S(1)} all-to-all(bf16[1024,3,256]{2,1,0:T(4,128)(2,1)S(1)} %pad_maximum_fusion), channel_id=1, replica_groups=mesh['seq'=4,'fsdp'=8] {'seq'}, dimensions={0} | all-to-all | bytes 3145728 | tf_op jit(solution)/shard_map/all_to_all | solution.py:39
  767.9 2.8 copy.105
  770.7 7.9 fusion.62
  778.7 29.1 %reduce-scatter.16.cloned.1.call-done = f32[32,16]{1,0:T(8,128)} async-done(((f32[1024,16]{1,0:T(8,128)}), f32[32,16]{1,0:T(8,128)}) %reduce-scatter.16.cloned.1.call-update) | async-done | bytes 2064
  809.2 11.6 %convolution_bitcast_fusion.1 = f32[2,1024,1024]{2,1,0:T(8,128)} fusion(bf16[8,2,128,1024]{3,2,0,1:T(8,128)(2,1)} %all-gather.10.cloned.1.call-done, bf16[8,2,128,1024]{3,2,0,1:T(8,128)(2,1)} %copy-done.39), kind=kOutput, calls=%fused_computation.41 | convolution fusion | flops 4294967296 | bytes 16777216 | tf_op jit(solution)/shard_map/sjcd,sjcf->jdf/dot_general | solution.py:175
  820.7 12.4 %convolution_bitcast_fusion = f32[2,1024,1024]{2,1,0:T(8,128)} fusion(bf16[8,2,128,1024]{3,2,0,1:T(8,128)(2,1)S(1)} %copy-done.37, f32[2,8,128,1024]{3,2,1,0:T(8,128)} %copy-done.38), kind=kOutput, calls=%fused_computation.40 | convolution fusion | flops 4313841664 | bytes 20971520 | tf_op jit(solution)/shard_map/sjcf,sjcd->jfd/dot_general | solution.py:171
  833.1 2.5 fusion.47
  835.7 37.6 %all-reduce.4 = (f32[1024]{0:T(1024)S(1)}, f32[1024]{0:T(1024)S(1)}) all-reduce(f32[1024]{0:T(1024)S(1)} %get-tuple-element.91, f32[1024]{0:T(1024)S(1)} %get-tuple-element.89), channel_id=4, replica_groups=mesh['seq'=4,'fsdp'=8] {'seq','fsdp'}, use_global_device_ids=true, to_apply=%region_21.22.clone | all-reduce | flops 2048 | bytes 16384
  875.7 74.1 %reduce-scatter.14.cloned.1.call-done = f32[32,1024]{1,0:T(8,128)} async-done(((f32[1024,1024]{1,0:T(8,128)}), f32[32,1024]{1,0:T(8,128)}) %reduce-scatter.14.cloned.1.call-update) | async-done | bytes 131088 | tf_op jit(solution)/shard_map/reduce_scatter | solution.py:234
  949.8 159.9 %reduce-scatter.12.cloned.1.call-done = f32[32,3072]{1,0:T(8,128)} async-done(((f32[1024,3072]{1,0:T(8,128)}), f32[32,3072]{1,0:T(8,128)}) %reduce-scatter.12.cloned.1.call-update) | async-done | bytes 393232 | tf_op jit(solution)/shard_map/reduce_scatter | solution.py:233
  (185 shorter events, 46.8 us)
Async XLA Ops:
  7.2 76.3 %all-gather.6.cloned.1.call-start = ((), (), s32[]{:S(2)}) async-start(), calls=%async_computation.13 | async-start | bytes 6488064 | tf_op jit(solution)/shard_map/all_gather | solution.py:88
  53.9 34.4 %copy-start.30 = (f32[256]{0:T(256)}, f32[256]{0:T(256)S(1)}, u32[]{:S(2)}) copy-start(f32[256]{0:T(256)S(1)} %fusion.48) | copy-start | bytes 3076
  53.9 34.4 %copy-start.28 = (f32[256]{0:T(256)}, f32[256]{0:T(256)S(1)}, u32[]{:S(2)}) copy-start(f32[256]{0:T(256)S(1)} %fusion.89) | copy-start | bytes 3076
  88.3 8.4 copy-start.22
  91.7 29.6 %all-to-all-start = ((bf16[256,3,1024]{0,1,2:T(4,128)(2,1)}), bf16[256,3,1024]{0,1,2:T(4,128)(2,1)S(1)}, u32[]{:S(2)}, u32[]{:S(2)}) async-start(bf16[256,3,1024]{0,1,2:T(4,128)(2,1)} %copy.83), calls=%async_computation | async-start | bytes 4194304 | tf_op jit(solution)/shard_map/all_to_all | solution.py:35
  95.3 72.9 %all-gather.8.cloned.1.call-start = ((), (), s32[]{:S(2)}) async-start(), calls=%async_computation.14 | async-start | bytes 2162688 | tf_op jit(solution)/shard_map/all_gather | solution.py:89
  127.4 6.8 copy-start.5
  129.8 4.4 copy-start.16
  130.0 10.7 copy-start.12
  131.7 6.6 copy-start
  135.8 4.9 copy-start.1
  138.3 4.8 copy-start.20
  140.7 27.5 %copy-start.8 = (bf16[1,256,1024]{2,1,0:T(8,128)(2,1)S(1)}, bf16[1,256,1024]{2,1,0:T(8,128)(2,1)}, u32[]{:S(2)}) copy-start(bf16[1,256,1024]{2,1,0:T(8,128)(2,1)} %param.27) | copy-start | bytes 1572868
  145.8 14.4 %all-to-all-start.1 = ((bf16[4,2,32768]{2,1,0:T(2,128)(2,1)}), bf16[4,2,32768]{2,1,0:T(2,128)(2,1)S(1)}, u32[]{:S(2)}, u32[]{:S(2)}) async-start(bf16[4,2,32768]{2,1,0:T(2,128)(2,1)} %reshape.434), calls=%async_computation.1 | async-start | bytes 1048576 | tf_op jit(solution)/shard_map/all_to_all | solution.py:39
  149.3 102.9 %all-gather.10.cloned.1.call-start = ((), (), s32[]{:S(2)}) async-start(), calls=%async_computation.15 | async-start | bytes 5242880 | tf_op jit(solution)/shard_map/all_gather | solution.py:51
  150.0 52.3 %copy-start.24 = (s32[256]{0:T(256)}, s32[256]{0:T(256)S(1)}, u32[]{:S(2)}) copy-start(s32[256]{0:T(256)S(1)} %add_add_fusion.2) | copy-start | bytes 3076
  162.9 97.0 %copy-start.14 = (bf16[256,1,4,256]{0,3,2,1:T(8,128)(2,1)}, bf16[256,1,4,256]{0,3,2,1:T(8,128)(2,1)S(1)}, u32[]{:S(2)}) copy-start(bf16[256,1,4,256]{0,3,2,1:T(8,128)(2,1)S(1)} %copy.91) | copy-start | bytes 1572868
  170.6 89.3 %copy-start.32 = (f32[256]{0:T(256)}, f32[256]{0:T(256)S(1)}, u32[]{:S(2)}) copy-start(f32[256]{0:T(256)S(1)} %get-tuple-element.113) | copy-start | bytes 3076
  170.6 89.3 %copy-start.26 = (f32[256]{0:T(256)}, f32[256]{0:T(256)S(1)}, u32[]{:S(2)}) copy-start(f32[256]{0:T(256)S(1)} %fusion.90) | copy-start | bytes 3076
  170.8 250.8 %copy-start.10 = (bf16[256,1024]{1,0:T(8,128)(2,1)}, bf16[256,1024]{1,0:T(8,128)(2,1)S(1)}, u32[]{:S(2)}) copy-start(bf16[256,1024]{1,0:T(8,128)(2,1)S(1)} %multiply_convert_fusion.3) | copy-start | bytes 1572868
  202.3 154.7 %reduce-scatter.8.cloned.1.call-start = ((), (), s32[]{:S(2)}) async-start(), calls=%async_computation.16 | async-start | bytes 10485760 | tf_op jit(solution)/shard_map/reduce_scatter | solution.py:55
  252.2 10.9 copy-start.35
  259.9 3.2 copy-start.38
  270.4 94.1 %copy-start.34 = (bf16[32,16]{0,1:T(8,128)(2,1)S(1)}, bf16[32,16]{0,1:T(8,128)(2,1)}, u32[]{:S(2)}) copy-start(bf16[32,16]{0,1:T(8,128)(2,1)} %param.34) | copy-start | bytes 3076
  270.4 152.3 %copy-start.18 = (bf16[1,256,1024]{2,1,0:T(8,128)(2,1)S(1)}, bf16[1,256,1024]{2,1,0:T(8,128)(2,1)}, u32[]{:S(2)}) copy-start(bf16[1,256,1024]{2,1,0:T(8,128)(2,1)} %param.37) | copy-start | bytes 1572868
  359.9 62.9 %all-to-all-start.3 = ((bf16[8,2,32,1024]{3,2,1,0:T(8,128)(2,1)}), bf16[8,2,32,1024]{3,2,1,0:T(8,128)(2,1)}, u32[]{:S(2)}, u32[]{:S(2)}) async-start(bf16[8,2,32,1024]{3,2,1,0:T(8,128)(2,1)} %copy.95), calls=%async_computation.4 | async-start | bytes 2097152 | tf_op jit(solution)/shard_map/all_to_all | solution.py:47
  364.5 143.7 %all-gather.12.cloned.1.call-start = ((), (), s32[]{:S(2)}) async-start(), calls=%async_computation.17 | async-start | bytes 5242880 | tf_op jit(solution)/shard_map/all_gather | solution.py:51
  457.5 159.6 %reduce-scatter.10.cloned.1.call-start = ((), (), s32[]{:S(2)}) async-start(), calls=%async_computation.18 | async-start | bytes 10485760 | tf_op jit(solution)/shard_map/reduce_scatter | solution.py:55
  508.2 15.5 %copy-start.36 = (bf16[2,1024,1024]{2,1,0:T(8,128)(2,1)S(1)}, bf16[2,1024,1024]{2,1,0:T(8,128)(2,1)}, u32[]{:S(2)}) copy-start(bf16[2,1024,1024]{2,1,0:T(8,128)(2,1)} %param.35) | copy-start | bytes 12582916
  521.6 2.1 copy-start.39
  530.5 94.3 %copy-start.19 = (bf16[1024,16]{0,1:T(8,128)(2,1)S(1)}, bf16[1024,16]{0,1:T(8,128)(2,1)}, u32[]{:S(2)}) copy-start(bf16[1024,16]{0,1:T(8,128)(2,1)} %reshape.426) | copy-start | bytes 98308
  530.5 94.3 %copy-start.23 = (s32[1,256,1]{1,2,0:T(1,128)S(1)}, s32[1,256,1]{1,2,0:T(1,128)}, u32[]{:S(2)}) copy-start(s32[1,256,1]{1,2,0:T(1,128)} %param.29) | copy-start | bytes 3076
  530.5 120.9 %copy-start.25 = (s32[256]{0:T(256)S(1)}, s32[256]{0:T(256)}, u32[]{:S(2)}) copy-start(s32[256]{0:T(256)} %copy-done.24) | copy-start | bytes 3076
  530.5 120.9 %copy-start.27 = (f32[256]{0:T(256)S(1)}, f32[256]{0:T(256)}, u32[]{:S(2)}) copy-start(f32[256]{0:T(256)} %copy-done.26) | copy-start | bytes 3076
  530.5 122.9 %copy-start.33 = (f32[256]{0:T(256)S(1)}, f32[256]{0:T(256)}, u32[]{:S(2)}) copy-start(f32[256]{0:T(256)} %copy-done.32) | copy-start | bytes 3076
  619.9 31.5 %all-to-all-start.5 = ((bf16[8,2,32,1024]{3,2,1,0:T(8,128)(2,1)}), bf16[8,2,32,1024]{3,2,1,0:T(8,128)(2,1)}, u32[]{:S(2)}, u32[]{:S(2)}) async-start(bf16[8,2,32,1024]{3,2,1,0:T(8,128)(2,1)} %copy.97), calls=%async_computation.7 | async-start | bytes 2097152 | tf_op jit(solution)/shard_map/all_to_all | solution.py:47
  651.4 4.8 copy-start.7
  666.7 12.3 %all-to-all-start.6 = ((bf16[4,2,32768]{2,1,0:T(2,128)(2,1)}), bf16[4,2,32768]{2,1,0:T(2,128)(2,1)}, u32[]{:S(2)}, u32[]{:S(2)}) async-start(bf16[4,2,32768]{2,1,0:T(2,128)(2,1)} %reshape.436), calls=%async_computation.8 | async-start | bytes 1048576 | tf_op jit(solution)/shard_map/all_to_all | solution.py:35
  670.8 136.9 %reduce-scatter.16.cloned.1.call-start = ((), (), s32[]{:S(2)}) async-start(), calls=%async_computation.21 | async-start | bytes 540672
  673.1 9.2 copy-start.21
  673.1 276.7 %reduce-scatter.14.cloned.1.call-start = ((), (), s32[]{:S(2)}) async-start(), calls=%async_computation.20 | async-start | bytes 4325376 | tf_op jit(solution)/shard_map/reduce_scatter | solution.py:234
  676.9 432.9 %reduce-scatter.12.cloned.1.call-start = ((), (), s32[]{:S(2)}) async-start(), calls=%async_computation.19 | async-start | bytes 12976128 | tf_op jit(solution)/shard_map/reduce_scatter | solution.py:233
  687.1 9.3 copy-start.13
  696.4 15.5 %slice-start = ((s8[8388608]{0:T(1024)(128)(4,1)}), s8[4194304]{0:T(1024)(128)(4,1)S(1)}, s32[]{:S(2)}) async-start(s8[8388608]{0:T(1024)(128)(4,1)} %bitcast.215), calls=%async_computation.22 | async-start | bytes 8388608
  696.4 15.5 %slice-start.2 = ((s8[8388608]{0:T(1024)(128)(4,1)}), s8[4194304]{0:T(1024)(128)(4,1)S(1)}, s32[]{:S(2)}) async-start(s8[8388608]{0:T(1024)(128)(4,1)} %bitcast.217), calls=%async_computation.24 | async-start | bytes 8388608
  704.2 7.7 slice-start.1
  704.2 8.2 slice-start.3
  712.4 10.4 copy-start.6
  720.8 2.0 copy-start.2
  720.8 3.4 copy-start.4
  724.2 6.7 copy-start.17
  727.6 3.5 copy-start.3
  727.6 6.3 copy-start.15
  734.0 36.7 %copy-start.9 = (bf16[1,256,1024]{2,1,0:T(8,128)(2,1)S(1)}, bf16[1,256,1024]{2,1,0:T(8,128)(2,1)}, u32[]{:S(2)}) copy-start(bf16[1,256,1024]{2,1,0:T(8,128)(2,1)} %param.27) | copy-start | bytes 1572868
  734.0 36.7 %copy-start.29 = (f32[256]{0:T(256)S(1)}, f32[256]{0:T(256)}, u32[]{:S(2)}) copy-start(f32[256]{0:T(256)} %copy-done.28) | copy-start | bytes 3076
  809.2 11.6 %copy-start.37 = (bf16[8,2,128,1024]{3,2,0,1:T(8,128)(2,1)S(1)}, bf16[8,2,128,1024]{3,2,0,1:T(8,128)(2,1)}, u32[]{:S(2)}) copy-start(bf16[8,2,128,1024]{3,2,0,1:T(8,128)(2,1)} %all-gather.12.cloned.1.call-done) | copy-start | bytes 12582916
  809.2 23.9 %slice-start.4 = ((s8[6291456]{0:T(1024)(128)(4,1)}), s8[4194304]{0:T(1024)(128)(4,1)S(1)}, s32[]{:S(2)}) async-start(s8[6291456]{0:T(1024)(128)(4,1)} %bitcast.257), calls=%async_computation.26 | async-start | bytes 8388608
  820.7 12.4 %copy-start.11 = (bf16[256,3,4,256]{0,3,2,1:T(8,128)(2,1)S(1)}, bf16[256,3,4,256]{0,3,2,1:T(8,128)(2,1)}, u32[]{:S(2)}) copy-start(bf16[256,3,4,256]{0,3,2,1:T(8,128)(2,1)} %copy.105) | copy-start | bytes 4718596
  820.7 12.4 %slice-start.5 = ((s8[6291456]{0:T(1024)(128)(4,1)}), s8[2097152]{0:T(1024)(128)(4,1)S(1)}, s32[]{:S(2)}) async-start(s8[6291456]{0:T(1024)(128)(4,1)} %bitcast.257), calls=%async_computation.27 | async-start | bytes 4194304
  833.1 41.3 %copy-start.31 = (f32[256]{0:T(256)S(1)}, f32[256]{0:T(256)}, u32[]{:S(2)}) copy-start(f32[256]{0:T(256)} %copy-done.30) | copy-start | bytes 3076
Sparse Core Ops, SparseCore 0:
  11.0 72.3 all-gather.5
  99.1 69.0 all-gather.7
  202.4 49.7 all-gather.9
  270.6 86.4 reduce-scatter.7
  457.6 50.5 all-gather.11
  530.6 86.3 reduce-scatter.9
  673.9 133.8 reduce-scatter.15
  810.7 139.0 reduce-scatter.13
  957.5 152.2 reduce-scatter.11
where the time goes:
time: 1120 us
  waiting for transfers between devices  634 us (57%)
  blocking collectives  224 us (20%)
  matrix products  133 us (12%)
  local copies, waits for them, and re-layouts  53.2 us (5%)
  other arithmetic  34.8 us (3%)
  starting transfers between devices  22.3 us (2%)
  between operations  15.5 us (1%)
    reduce_scatter x2, waiting for transfers between devices, collect_rows(): return lax.psum_scatter(value, 'seq', scatter_dimension=2, tiled=True)  173 us
    reduce_scatter x1, waiting for transfers between devices, shards(): lax.psum_scatter(grad_qkv_weight, ('seq', 'fsdp'), scatter_dimension=0, t...  160 us
    all_gather x2, waiting for transfers between devices, spread_rows(): return lax.all_gather(value, 'seq', axis=2, tiled=True)  99.9 us
    unnamed x2, blocking collectives  80.7 us
    reduce_scatter x1, waiting for transfers between devices, shards(): lax.psum_scatter(grad_mix, ('seq', 'fsdp'), scatter_dimension=0, tiled=True)  74.1 us
    all_to_all x2, blocking collectives, to_owners(): lax.all_to_all(value, 'fsdp', split_axis=0, concat_axis=0, tiled=True)  59 us
    all_gather x1, blocking collectives, shards(): lax.all_gather(router_weight, ('seq', 'fsdp'), axis=0, tiled=True)  56.3 us
    unnamed x10, waiting for transfers between devices  30.3 us
  transfers between devices with their start and end apart: 14, of which 13 were waited for; matrix products, arithmetic and copies ran while one was open for 12% of the time, Pallas kernels for 0%

commit v1 on v0

--- a/solution.py
+++ b/solution.py
@@ -134,8 +134,9 @@
         return jnp.sum(jnp.where(choose, jax.nn.softmax(logit_rows, axis=-1), 0.0), axis=-1)
 
     gate, gate_back = jax.vjp(gate_of, logits)
-    counts = choose.astype(jnp.int32)
-    ranks = jnp.sum(jnp.cumsum(counts, axis=0) * counts, axis=1) - 1
+    order = jnp.arange(tokens, dtype=jnp.int32)
+    earlier = (order[None, :] < order[:, None]) & (chosen[None, :] == chosen[:, None])
+    ranks = jnp.sum(earlier.astype(jnp.int32), axis=1)
     slot = chosen * capacity + ranks
     dispatch = (
         jnp.arange(experts_all * capacity, dtype=jnp.int32)[:, None] == slot[None, :]

time: 1120 us -> 1120 us (level)
  no operation moved by 1% of the time
where the time goes in v1:
time: 1120 us
  waiting for transfers between devices  635 us (57%)
  blocking collectives  224 us (20%)
  matrix products  133 us (12%)
  local copies, waits for them, and re-layouts  53 us (5%)
  other arithmetic  34.3 us (3%)
  starting transfers between devices  22.3 us (2%)
  between operations  15.5 us (1%)
    reduce_scatter x2, waiting for transfers between devices, collect_rows(): return lax.psum_scatter(value, 'seq', scatter_dimension=2, tiled=True)  173 us
    reduce_scatter x1, waiting for transfers between devices, shards(): lax.psum_scatter(grad_qkv_weight, ('seq', 'fsdp'), scatter_dimension=0, t...  160 us
    all_gather x2, waiting for transfers between devices, spread_rows(): return lax.all_gather(value, 'seq', axis=2, tiled=True)  99.9 us
    unnamed x2, blocking collectives  80.7 us
    reduce_scatter x1, waiting for transfers between devices, shards(): lax.psum_scatter(grad_mix, ('seq', 'fsdp'), scatter_dimension=0, tiled=True)  73.6 us
    all_to_all x2, blocking collectives, to_owners(): lax.all_to_all(value, 'fsdp', split_axis=0, concat_axis=0, tiled=True)  59 us
    all_gather x1, blocking collectives, shards(): lax.all_gather(router_weight, ('seq', 'fsdp'), axis=0, tiled=True)  56.3 us
    unnamed x10, waiting for transfers between devices  30.3 us
  transfers between devices with their start and end apart: 14, of which 13 were waited for; matrix products, arithmetic and copies ran while one was open for 12% of the time, Pallas kernels for 0%

profile of v1, /device:TPU:0, one launch (start us, length us, event | category | flops | bytes accessed | tf_op | source)
XLA Modules:
  0.0 1116.4 jit_solution(17351588025040472665)
XLA Ops:
  9.6 43.1 %all-reduce.5 = (bf16[1024]{0:T(1024)(128)(2,1)S(1)}, bf16[1024]{0:T(1024)(128)(2,1)S(1)}) all-reduce(bf16[1024]{0:T(1024)(128)(2,1)S(1)} %dynamic-update-slice.8, bf16[1024]{0:T(1024)(128)(2,1)S(1)} %dynamic-update-slice.9), channel_id=1, replica_groups=mesh['seq'=4,'fsdp'=8] {'seq','fsdp'}, use_global_device_ids=true, to_apply=%add | all-reduce | flops 2048 | bytes 8192
  53.9 29.5 %all-gather.6.cloned.1.call-done = bf16[1024,3072]{1,0:T(8,128)(2,1)} async-done(((bf16[32,3072]{1,0:T(8,128)(2,1)}), bf16[1024,3072]{1,0:T(8,128)(2,1)}) %all-gather.6.cloned.1.call-update) | async-done | bytes 6291472 | tf_op jit(solution)/shard_map/all_gather | solution.py:88
  83.4 4.8 convolution_convert_fusion
  89.0 2.7 copy.103
  91.7 3.6 all-to-all-start
  97.3 24.1 %all-to-all-done = bf16[256,3,1024]{0,1,2:T(4,128)(2,1)S(1)} async-done(((bf16[256,3,1024]{0,1,2:T(4,128)(2,1)}), bf16[256,3,1024]{0,1,2:T(4,128)(2,1)S(1)}, u32[]{:S(2)}, u32[]{:S(2)}) %all-to-all-start) | async-done | bytes 1572896 | tf_op jit(solution)/shard_map/all_to_all | solution.py:35
  131.7 2.4 exponential_reduce_fusion
  135.8 2.4 exponential_reduce_fusion.1
  138.3 2.4 fusion.43
  140.7 2.4 fusion.42
  145.8 3.5 all-to-all-start.1
  149.9 10.4 all-to-all-done.1
  162.9 5.3 all-gather.8.cloned.1.call-done
  168.2 2.4 multiply_reduce_fusion.4
  171.3 29.9 %all_to_all.83 = bf16[8,2,32,1024]{3,2,1,0:T(8,128)(2,1)S(1)} all-to-all(bf16[8,2,32,1024]{3,2,1,0:T(8,128)(2,1)S(1)} %bitcast.222), channel_id=1, replica_groups=mesh['seq'=4,'fsdp'=8] {'fsdp'}, dimensions={0} | all-to-all | bytes 2097152 | tf_op jit(solution)/shard_map/all_to_all | solution.py:43
  202.4 49.8 %all-gather.10.cloned.1.call-done = bf16[8,2,128,1024]{3,2,0,1:T(8,128)(2,1)} async-done(((bf16[8,2,32,1024]{3,2,0,1:T(8,128)(2,1)}), bf16[8,2,128,1024]{3,2,0,1:T(8,128)(2,1)}) %all-gather.10.cloned.1.call-update) | async-done | bytes 4194320 | tf_op jit(solution)/shard_map/all_gather | solution.py:51
  252.2 7.7 fusion.17
  259.9 3.2 copy-done.38
  263.1 7.3 fusion.22
  270.4 86.6 %reduce-scatter.8.cloned.1.call-done = f32[8,2,32,1024]{3,2,0,1:T(8,128)} async-done(((f32[8,2,128,1024]{3,2,0,1:T(8,128)}), f32[8,2,32,1024]{3,2,0,1:T(8,128)}) %reduce-scatter.8.cloned.1.call-update) | async-done | bytes 2097168 | tf_op jit(solution)/shard_map/reduce_scatter | solution.py:55
  357.0 1.7 convert_element_type.124
  359.8 4.6 all-to-all-start.3
  364.5 56.3 %all-gather = bf16[32,32,16]{1,2,0:T(8,128)(2,1)S(1)} all-gather(bf16[1,32,16]{1,2,0:T(8,128)(2,1)S(1)} %bitcast.239), channel_id=1, replica_groups=mesh['seq'=4,'fsdp'=8] {'seq','fsdp'}, dimensions={0}, use_global_device_ids=true | all-gather | bytes 33792 | tf_op jit(solution)/shard_map/all_gather | solution.py:91
  422.7 2.7 fusion.57
  427.3 29.0 %all_to_all.84 = bf16[8,2,32,1024]{3,2,1,0:T(8,128)(2,1)S(1)} all-to-all(bf16[8,2,32,1024]{3,2,1,0:T(8,128)(2,1)S(1)} %bitcast.232), channel_id=1, replica_groups=mesh['seq'=4,'fsdp'=8] {'fsdp'}, dimensions={0} | all-to-all | bytes 2097152 | tf_op jit(solution)/shard_map/all_to_all | solution.py:43
  458.0 50.1 %all-gather.12.cloned.1.call-done = bf16[8,2,128,1024]{3,2,0,1:T(8,128)(2,1)} async-done(((bf16[8,2,32,1024]{3,2,0,1:T(8,128)(2,1)}), bf16[8,2,128,1024]{3,2,0,1:T(8,128)(2,1)}) %all-gather.12.cloned.1.call-update) | async-done | bytes 4194320 | tf_op jit(solution)/shard_map/all_gather | solution.py:51
  508.1 13.4 %fusion.6 = bf16[8,2,128,1024]{3,2,0,1:T(8,128)(2,1)S(1)} fusion(f32[2,8,128,1024]{3,2,1,0:T(8,128)} %copy-done.38, bf16[8,2,128,1024]{3,2,0,1:T(8,128)(2,1)} %all-gather.12.cloned.1.call-done, bf16[2,1024,1024]{2,1,0:T(8,128)(2,1)} %param.36), kind=kOutput, calls=%fused_computation.8 | convolution fusion | flops 4336910336 | bytes 20971520 | tf_op jit(solution)/shard_map/sjcd,jfd->sjcf/dot_general | solution.py:169
  521.5 2.1 copy-done.39
  523.6 6.8 fusion.25
  530.4 86.6 %reduce-scatter.10.cloned.1.call-done = f32[8,2,32,1024]{3,2,0,1:T(8,128)} async-done(((f32[8,2,128,1024]{3,2,0,1:T(8,128)}), f32[8,2,32,1024]{3,2,0,1:T(8,128)}) %reduce-scatter.10.cloned.1.call-update) | async-done | bytes 2097168 | tf_op jit(solution)/shard_map/reduce_scatter | solution.py:55
  617.0 1.7 convert_element_type.132
  619.8 4.8 all-to-all-start.5
  625.0 26.3 %all-to-all-done.5 = bf16[8,2,32,1024]{3,2,1,0:T(8,128)(2,1)} async-done(((bf16[8,2,32,1024]{3,2,1,0:T(8,128)(2,1)}), bf16[8,2,32,1024]{3,2,1,0:T(8,128)(2,1)}, u32[]{:S(2)}, u32[]{:S(2)}) %all-to-all-start.5) | async-done | bytes 1048608 | tf_op jit(solution)/shard_map/all_to_all | solution.py:47
  651.3 2.1 multiply_reduce_fusion.2
  653.4 2.7 fusion.52
  657.6 2.4 copy.117
  660.0 4.6 reduce.9
  664.7 2.0 reshape.418
  666.6 4.1 all-to-all-start.6
  670.8 2.2 fusion.89
  673.1 3.7 fusion.73
  677.1 1.9 all-to-all-done.6
  678.9 2.2 reshape.419
  682.2 4.8 fusion.95
  687.0 5.7 fusion.36
  692.7 3.6 copy.122
  696.3 7.8 multiply_reduce_fusion
  704.1 7.7 multiply_reduce_fusion.1
  712.3 8.4 multiply_convert_fusion
  720.7 2.0 copy-done.2
  725.6 2.0 copy.120
  727.6 3.2 fusion.104
  731.9 2.0 copy.121
  733.9 4.9 pad_maximum_fusion
  738.8 27.6 %all_to_all.85 = bf16[1024,3,256]{2,1,0:T(4,128)(2,1)S(1)} all-to-all(bf16[1024,3,256]{2,1,0:T(4,128)(2,1)S(1)} %pad_maximum_fusion), channel_id=1, replica_groups=mesh['seq'=4,'fsdp'=8] {'seq'}, dimensions={0} | all-to-all | bytes 3145728 | tf_op jit(solution)/shard_map/all_to_all | solution.py:39
  767.8 2.8 copy.124
  770.7 7.9 fusion.62
  778.7 29.0 %reduce-scatter.16.cloned.1.call-done = f32[32,16]{1,0:T(8,128)} async-done(((f32[1024,16]{1,0:T(8,128)}), f32[32,16]{1,0:T(8,128)}) %reduce-scatter.16.cloned.1.call-update) | async-done | bytes 2064
  809.1 11.6 %convolution_bitcast_fusion.1 = f32[2,1024,1024]{2,1,0:T(8,128)} fusion(bf16[8,2,128,1024]{3,2,0,1:T(8,128)(2,1)} %all-gather.10.cloned.1.call-done, bf16[8,2,128,1024]{3,2,0,1:T(8,128)(2,1)} %copy-done.39), kind=kOutput, calls=%fused_computation.41 | convolution fusion | flops 4294967296 | bytes 16777216 | tf_op jit(solution)/shard_map/sjcd,sjcf->jdf/dot_general | solution.py:176
  820.7 12.4 %convolution_bitcast_fusion = f32[2,1024,1024]{2,1,0:T(8,128)} fusion(bf16[8,2,128,1024]{3,2,0,1:T(8,128)(2,1)S(1)} %copy-done.37, f32[2,8,128,1024]{3,2,1,0:T(8,128)} %copy-done.38), kind=kOutput, calls=%fused_computation.40 | convolution fusion | flops 4313841664 | bytes 20971520 | tf_op jit(solution)/shard_map/sjcf,sjcd->jfd/dot_general | solution.py:172
  833.1 2.5 fusion.47
  835.6 37.6 %all-reduce.4 = (f32[1024]{0:T(1024)S(1)}, f32[1024]{0:T(1024)S(1)}) all-reduce(f32[1024]{0:T(1024)S(1)} %get-tuple-element.91, f32[1024]{0:T(1024)S(1)} %get-tuple-element.89), channel_id=4, replica_groups=mesh['seq'=4,'fsdp'=8] {'seq','fsdp'}, use_global_device_ids=true, to_apply=%region_19.20.clone | all-reduce | flops 2048 | bytes 16384
  875.7 73.6 %reduce-scatter.14.cloned.1.call-done = f32[32,1024]{1,0:T(8,128)} async-done(((f32[1024,1024]{1,0:T(8,128)}), f32[32,1024]{1,0:T(8,128)}) %reduce-scatter.14.cloned.1.call-update) | async-done | bytes 131088 | tf_op jit(solution)/shard_map/reduce_scatter | solution.py:235
  949.3 160.5 %reduce-scatter.12.cloned.1.call-done = f32[32,3072]{1,0:T(8,128)} async-done(((f32[1024,3072]{1,0:T(8,128)}), f32[32,3072]{1,0:T(8,128)}) %reduce-scatter.12.cloned.1.call-update) | async-done | bytes 393232 | tf_op jit(solution)/shard_map/reduce_scatter | solution.py:234
  (180 shorter events, 46.0 us)
Async XLA Ops:
  7.2 76.3 %all-gather.6.cloned.1.call-start = ((), (), s32[]{:S(2)}) async-start(), calls=%async_computation.13 | async-start | bytes 6488064 | tf_op jit(solution)/shard_map/all_gather | solution.py:88
  53.9 34.4 %copy-start.30 = (f32[256]{0:T(256)}, f32[256]{0:T(256)S(1)}, u32[]{:S(2)}) copy-start(f32[256]{0:T(256)S(1)} %fusion.48) | copy-start | bytes 3076
  53.9 34.4 %copy-start.28 = (f32[256]{0:T(256)}, f32[256]{0:T(256)S(1)}, u32[]{:S(2)}) copy-start(f32[256]{0:T(256)S(1)} %fusion.87) | copy-start | bytes 3076
  91.7 29.6 %all-to-all-start = ((bf16[256,3,1024]{0,1,2:T(4,128)(2,1)}), bf16[256,3,1024]{0,1,2:T(4,128)(2,1)S(1)}, u32[]{:S(2)}, u32[]{:S(2)}) async-start(bf16[256,3,1024]{0,1,2:T(4,128)(2,1)} %copy.103), calls=%async_computation | async-start | bytes 4194304 | tf_op jit(solution)/shard_map/all_to_all | solution.py:35
  95.3 72.9 %all-gather.8.cloned.1.call-start = ((), (), s32[]{:S(2)}) async-start(), calls=%async_computation.14 | async-start | bytes 2162688 | tf_op jit(solution)/shard_map/all_gather | solution.py:89
  127.3 6.8 copy-start.5
  129.7 4.4 copy-start.16
  130.0 10.7 copy-start.12
  131.7 6.6 copy-start
  135.8 4.9 copy-start.1
  138.3 4.8 copy-start.20
  140.7 9.0 copy-start.22
  140.7 27.5 %copy-start.8 = (bf16[1,256,1024]{2,1,0:T(8,128)(2,1)S(1)}, bf16[1,256,1024]{2,1,0:T(8,128)(2,1)}, u32[]{:S(2)}) copy-start(bf16[1,256,1024]{2,1,0:T(8,128)(2,1)} %param.27) | copy-start | bytes 1572868
  145.8 14.4 %all-to-all-start.1 = ((bf16[4,2,32768]{2,1,0:T(2,128)(2,1)}), bf16[4,2,32768]{2,1,0:T(2,128)(2,1)S(1)}, u32[]{:S(2)}, u32[]{:S(2)}) async-start(bf16[4,2,32768]{2,1,0:T(2,128)(2,1)} %reshape.416), calls=%async_computation.1 | async-start | bytes 1048576 | tf_op jit(solution)/shard_map/all_to_all | solution.py:39
  149.3 102.9 %all-gather.10.cloned.1.call-start = ((), (), s32[]{:S(2)}) async-start(), calls=%async_computation.15 | async-start | bytes 5242880 | tf_op jit(solution)/shard_map/all_gather | solution.py:51
  149.9 52.4 %copy-start.24 = (s32[256]{0:T(256)}, s32[256]{0:T(256)S(1)}, u32[]{:S(2)}) copy-start(s32[256]{0:T(256)S(1)} %multiply_add_fusion) | copy-start | bytes 3076
  162.9 97.0 %copy-start.14 = (bf16[256,1,4,256]{0,3,2,1:T(8,128)(2,1)}, bf16[256,1,4,256]{0,3,2,1:T(8,128)(2,1)S(1)}, u32[]{:S(2)}) copy-start(bf16[256,1,4,256]{0,3,2,1:T(8,128)(2,1)S(1)} %copy.111) | copy-start | bytes 1572868
  170.6 89.3 %copy-start.32 = (f32[256]{0:T(256)}, f32[256]{0:T(256)S(1)}, u32[]{:S(2)}) copy-start(f32[256]{0:T(256)S(1)} %get-tuple-element.113) | copy-start | bytes 3076
  170.6 89.3 %copy-start.26 = (f32[256]{0:T(256)}, f32[256]{0:T(256)S(1)}, u32[]{:S(2)}) copy-start(f32[256]{0:T(256)S(1)} %fusion.88) | copy-start | bytes 3076
  170.8 250.8 %copy-start.10 = (bf16[256,1024]{1,0:T(8,128)(2,1)}, bf16[256,1024]{1,0:T(8,128)(2,1)S(1)}, u32[]{:S(2)}) copy-start(bf16[256,1024]{1,0:T(8,128)(2,1)S(1)} %multiply_convert_fusion.3) | copy-start | bytes 1572868
  202.3 154.7 %reduce-scatter.8.cloned.1.call-start = ((), (), s32[]{:S(2)}) async-start(), calls=%async_computation.16 | async-start | bytes 10485760 | tf_op jit(solution)/shard_map/reduce_scatter | solution.py:55
  252.2 10.9 copy-start.35
  259.9 3.2 copy-start.38
  270.4 94.1 %copy-start.34 = (bf16[32,16]{0,1:T(8,128)(2,1)S(1)}, bf16[32,16]{0,1:T(8,128)(2,1)}, u32[]{:S(2)}) copy-start(bf16[32,16]{0,1:T(8,128)(2,1)} %param.34) | copy-start | bytes 3076
  270.4 152.3 %copy-start.18 = (bf16[1,256,1024]{2,1,0:T(8,128)(2,1)S(1)}, bf16[1,256,1024]{2,1,0:T(8,128)(2,1)}, u32[]{:S(2)}) copy-start(bf16[1,256,1024]{2,1,0:T(8,128)(2,1)} %param.37) | copy-start | bytes 1572868
  359.8 62.9 %all-to-all-start.3 = ((bf16[8,2,32,1024]{3,2,1,0:T(8,128)(2,1)}), bf16[8,2,32,1024]{3,2,1,0:T(8,128)(2,1)}, u32[]{:S(2)}, u32[]{:S(2)}) async-start(bf16[8,2,32,1024]{3,2,1,0:T(8,128)(2,1)} %copy.114), calls=%async_computation.4 | async-start | bytes 2097152 | tf_op jit(solution)/shard_map/all_to_all | solution.py:47
  364.5 143.6 %all-gather.12.cloned.1.call-start = ((), (), s32[]{:S(2)}) async-start(), calls=%async_computation.17 | async-start | bytes 5242880 | tf_op jit(solution)/shard_map/all_gather | solution.py:51
  457.4 159.6 %reduce-scatter.10.cloned.1.call-start = ((), (), s32[]{:S(2)}) async-start(), calls=%async_computation.18 | async-start | bytes 10485760 | tf_op jit(solution)/shard_map/reduce_scatter | solution.py:55
  508.1 15.5 %copy-start.36 = (bf16[2,1024,1024]{2,1,0:T(8,128)(2,1)S(1)}, bf16[2,1024,1024]{2,1,0:T(8,128)(2,1)}, u32[]{:S(2)}) copy-start(bf16[2,1024,1024]{2,1,0:T(8,128)(2,1)} %param.35) | copy-start | bytes 12582916
  521.5 2.1 copy-start.39
  530.4 94.3 %copy-start.19 = (bf16[1024,16]{0,1:T(8,128)(2,1)S(1)}, bf16[1024,16]{0,1:T(8,128)(2,1)}, u32[]{:S(2)}) copy-start(bf16[1024,16]{0,1:T(8,128)(2,1)} %reshape.409) | copy-start | bytes 98308
  530.4 94.3 %copy-start.23 = (s32[1,256,1]{1,2,0:T(1,128)S(1)}, s32[1,256,1]{1,2,0:T(1,128)}, u32[]{:S(2)}) copy-start(s32[1,256,1]{1,2,0:T(1,128)} %param.29) | copy-start | bytes 3076
  530.4 120.9 %copy-start.25 = (s32[256]{0:T(256)S(1)}, s32[256]{0:T(256)}, u32[]{:S(2)}) copy-start(s32[256]{0:T(256)} %copy-done.24) | copy-start | bytes 3076
  530.4 120.9 %copy-start.27 = (f32[256]{0:T(256)S(1)}, f32[256]{0:T(256)}, u32[]{:S(2)}) copy-start(f32[256]{0:T(256)} %copy-done.26) | copy-start | bytes 3076
  530.4 122.9 %copy-start.33 = (f32[256]{0:T(256)S(1)}, f32[256]{0:T(256)}, u32[]{:S(2)}) copy-start(f32[256]{0:T(256)} %copy-done.32) | copy-start | bytes 3076
  619.8 31.5 %all-to-all-start.5 = ((bf16[8,2,32,1024]{3,2,1,0:T(8,128)(2,1)}), bf16[8,2,32,1024]{3,2,1,0:T(8,128)(2,1)}, u32[]{:S(2)}, u32[]{:S(2)}) async-start(bf16[8,2,32,1024]{3,2,1,0:T(8,128)(2,1)} %copy.116), calls=%async_computation.7 | async-start | bytes 2097152 | tf_op jit(solution)/shard_map/all_to_all | solution.py:47
  651.3 4.8 copy-start.7
  666.6 12.3 %all-to-all-start.6 = ((bf16[4,2,32768]{2,1,0:T(2,128)(2,1)}), bf16[4,2,32768]{2,1,0:T(2,128)(2,1)}, u32[]{:S(2)}, u32[]{:S(2)}) async-start(bf16[4,2,32768]{2,1,0:T(2,128)(2,1)} %reshape.418), calls=%async_computation.8 | async-start | bytes 1048576 | tf_op jit(solution)/shard_map/all_to_all | solution.py:35
  670.8 136.9 %reduce-scatter.16.cloned.1.call-start = ((), (), s32[]{:S(2)}) async-start(), calls=%async_computation.21 | async-start | bytes 540672
  673.0 9.2 copy-start.21
  673.0 276.2 %reduce-scatter.14.cloned.1.call-start = ((), (), s32[]{:S(2)}) async-start(), calls=%async_computation.20 | async-start | bytes 4325376 | tf_op jit(solution)/shard_map/reduce_scatter | solution.py:235
  676.8 433.0 %reduce-scatter.12.cloned.1.call-start = ((), (), s32[]{:S(2)}) async-start(), calls=%async_computation.19 | async-start | bytes 12976128 | tf_op jit(solution)/shard_map/reduce_scatter | solution.py:234
  687.0 9.3 copy-start.13
  696.3 15.5 %slice-start = ((s8[8388608]{0:T(1024)(128)(4,1)}), s8[4194304]{0:T(1024)(128)(4,1)S(1)}, s32[]{:S(2)}) async-start(s8[8388608]{0:T(1024)(128)(4,1)} %bitcast.199), calls=%async_computation.22 | async-start | bytes 8388608
  696.3 15.5 %slice-start.2 = ((s8[8388608]{0:T(1024)(128)(4,1)}), s8[4194304]{0:T(1024)(128)(4,1)S(1)}, s32[]{:S(2)}) async-start(s8[8388608]{0:T(1024)(128)(4,1)} %bitcast.201), calls=%async_computation.24 | async-start | bytes 8388608
  704.1 7.7 slice-start.1
  704.1 8.2 slice-start.3
  712.3 10.4 copy-start.6
  720.7 2.0 copy-start.2
  720.7 3.4 copy-start.4
  724.1 6.7 copy-start.17
  727.6 3.5 copy-start.3
  727.6 6.3 copy-start.15
  733.9 36.8 %copy-start.9 = (bf16[1,256,1024]{2,1,0:T(8,128)(2,1)S(1)}, bf16[1,256,1024]{2,1,0:T(8,128)(2,1)}, u32[]{:S(2)}) copy-start(bf16[1,256,1024]{2,1,0:T(8,128)(2,1)} %param.27) | copy-start | bytes 1572868
  733.9 36.8 %copy-start.29 = (f32[256]{0:T(256)S(1)}, f32[256]{0:T(256)}, u32[]{:S(2)}) copy-start(f32[256]{0:T(256)} %copy-done.28) | copy-start | bytes 3076
  809.1 11.6 %copy-start.37 = (bf16[8,2,128,1024]{3,2,0,1:T(8,128)(2,1)S(1)}, bf16[8,2,128,1024]{3,2,0,1:T(8,128)(2,1)}, u32[]{:S(2)}) copy-start(bf16[8,2,128,1024]{3,2,0,1:T(8,128)(2,1)} %all-gather.12.cloned.1.call-done) | copy-start | bytes 12582916
  809.1 23.9 %slice-start.4 = ((s8[6291456]{0:T(1024)(128)(4,1)}), s8[4194304]{0:T(1024)(128)(4,1)S(1)}, s32[]{:S(2)}) async-start(s8[6291456]{0:T(1024)(128)(4,1)} %bitcast.240), calls=%async_computation.26 | async-start | bytes 8388608
  820.7 12.4 %copy-start.11 = (bf16[256,3,4,256]{0,3,2,1:T(8,128)(2,1)S(1)}, bf16[256,3,4,256]{0,3,2,1:T(8,128)(2,1)}, u32[]{:S(2)}) copy-start(bf16[256,3,4,256]{0,3,2,1:T(8,128)(2,1)} %copy.124) | copy-start | bytes 4718596
  820.7 12.4 %slice-start.5 = ((s8[6291456]{0:T(1024)(128)(4,1)}), s8[2097152]{0:T(1024)(128)(4,1)S(1)}, s32[]{:S(2)}) async-start(s8[6291456]{0:T(1024)(128)(4,1)} %bitcast.240), calls=%async_computation.27 | async-start | bytes 4194304
  833.1 41.3 %copy-start.31 = (f32[256]{0:T(256)S(1)}, f32[256]{0:T(256)}, u32[]{:S(2)}) copy-start(f32[256]{0:T(256)} %copy-done.30) | copy-start | bytes 3076
Sparse Core Ops, SparseCore 0:
  11.0 72.3 all-gather.5
  99.1 69.0 all-gather.7
  202.4 49.7 all-gather.9
  270.6 86.4 reduce-scatter.7
  457.5 50.5 all-gather.11
  530.5 86.4 reduce-scatter.9
  673.9 133.8 reduce-scatter.15
  810.7 138.5 reduce-scatter.13
  956.9 152.7 reduce-scatter.11

commit v2 on v0

v2 whole, which is shorter than its diff:
```python
import functools

import jax
import jax.numpy as jnp
from jax import lax
from jax.experimental import pallas as pl
from jax.experimental.pallas import tpu as pltpu
from jax.sharding import PartitionSpec as P

HEAD_DIM = 64
QBLOCK = 512
EPS = 1e-05
MASKED = -1e30
MESH = pl.DeviceIdType.MESH
ANY = pl.BlockSpec(memory_space=pl.ANY)


def scaled_norm(value, gain):
    return value * lax.rsqrt(jnp.mean(value * value, axis=-1, keepdims=True) + EPS) * gain


def gelu_tanh(value):
    return jax.nn.gelu(value, approximate=True)


def times(left, right):
    return jnp.dot(left, right, preferred_element_type=jnp.float32)


def times_transposed(left, right):
    return lax.dot_general(
        left, right, (((1,), (1,)), ((), ())), preferred_element_type=jnp.float32
    )


def transposed_times(left, right):
    return lax.dot_general(
        left, right, (((0,), (0,)), ((), ())), preferred_element_type=jnp.float32
    )


def greet(axis, peers):
    barrier = pltpu.get_barrier_semaphore()
    for peer in peers:
        pl.semaphore_signal(barrier, inc=1, device_id={axis: peer}, device_id_type=MESH)
    pl.semaphore_wait(barrier, len(peers))


def remote(axis, peer, source, target, send, receive):
    copy = pltpu.make_async_remote_copy(
        source, target, send, receive, device_id={axis: peer}, device_id_type=MESH
    )
    copy.start()
    return copy


def call(kernel, inputs, outputs, scratch, number):
    return pl.pallas_call(
        kernel,
        out_shape=outputs,
        in_specs=[ANY] * len(inputs),
        out_specs=jax.tree.map(lambda _: ANY, outputs),
        scratch_shapes=scratch,
        compiler_params=pltpu.CompilerParams(
            collective_id=number, has_side_effects=True, vmem_limit_bytes=48 * 2**20
        ),
    )(*inputs)


def exchange_kernel(axis, count, views, *refs):
    arrays = len(views)
    sources, targets = refs[:arrays], refs[arrays : 2 * arrays]
    send, receive, local = refs[2 * arrays :]
    me = lax.axis_index(axis)
    peers = [lax.rem(me + step, count) for step in range(1, count)]
    greet(axis, peers)
    copies = []
    for step, peer in enumerate(peers):
        for a, (out_of, into) in enumerate(views):
            copies.append(
                remote(
                    axis,
                    peer,
                    out_of(sources[a], peer),
                    into(targets[a], me),
                    send.at[a, step],
                    receive.at[a, step],
                )
            )
    for a, (out_of, into) in enumerate(views):
        copy = pltpu.make_async_copy(out_of(sources[a], me), into(targets[a], me), local.at[a])
        copy.start()
        copies.append(copy)
    for copy in copies:
        copy.wait()


def exchange(axis, count, inputs, outputs, views, number):
    arrays = len(views)
    return call(
        functools.partial(exchange_kernel, axis, count, views),
        inputs,
        outputs,
        [
            pltpu.SemaphoreType.DMA((arrays, count - 1)),
            pltpu.SemaphoreType.DMA((arrays, count - 1)),
            pltpu.SemaphoreType.DMA((arrays,)),
        ],
        number,
    )


def lead(ref, place):
    return ref.at[place]


def second(ref, place):
    return ref.at[:, place]


def whole(ref, place):
    return ref


def spread_kernel(source, target, send, receive, local):
    me = lax.axis_index("seq")
    one, two, both = me ^ 1, me ^ 2, me ^ 3
    half = source.shape[1] // 2
    greet("seq", [one, two])
    parts = (pl.ds(0, half), pl.ds(half, half))
    own = pltpu.make_async_copy(source, target.at[:, me], local)
    own.start()
    copies = {}
    for side, peer in enumerate((one, two)):
        for order in range(2):
            part = (order + side) % 2
            copies[side, part] = remote(
                "seq",
                peer,
                source.at[:, parts[part]],
                target.at[:, me, parts[part]],
                send.at[side, part],
                receive.at[side, part],
            )
    relayed = []
    for side, (origin, peer) in enumerate(((one, two), (two, one))):
        copies[side, side].wait_recv()
        block = target.at[:, origin, parts[side]]
        relayed.append(remote("seq", peer, block, block, send.at[2, side], receive.at[2, side]))
    for side in range(2):
        copies[side, 1 - side].wait_recv()
        for part in range(2):
            copies[side, part].wait_send()
    for copy in relayed:
        copy.wait()
    own.wait()


def spread(source, number):
    return call(
        spread_kernel,
        (source,),
        jax.ShapeDtypeStruct((source.shape[0], 4, *source.shape[1:]), source.dtype),
        [
            pltpu.SemaphoreType.DMA((3, 2)),
            pltpu.SemaphoreType.DMA((3, 2)),
            pltpu.SemaphoreType.DMA,
        ],
        number,
    )


def columns_kernel(count, source, target, staged, send, receive, local, far_send, far_receive, near_send, near_receive):
    me, place = lax.axis_index("seq"), lax.axis_index("fsdp")
    barrier = pltpu.get_barrier_semaphore()
    others = [lax.rem(me + step, 4) for step in range(1, 4)]
    sibling = place ^ 1
    chips = count // 2
    chip, core = place // 2, lax.rem(place, 2)
    far = [lax.rem(chip + step, chips) * 2 + core for step in range(1, chips)]
    for other in others:
        pl.semaphore_signal(barrier, inc=1, device_id={"seq": other}, device_id_type=MESH)
    for other in [sibling, *far]:
        pl.semaphore_signal(barrier, inc=1, device_id={"fsdp": other}, device_id_type=MESH)
    pl.semaphore_wait(barrier, 3 + chips)
    copies = []
    for step, other in enumerate(others):
        copies.append(
            remote("seq", other, source.at[other], staged.at[me], send.at[step], receive.at[step])
        )
    own = pltpu.make_async_copy(source.at[me], staged.at[me], local.at[0])
    own.start()
    own.wait()
    for copy in copies:
        copy.wait()
    block = target.at[:, place]
    keep = pltpu.make_async_copy(staged, block, local.at[1])
    keep.start()
    away = [
        remote("fsdp", other, staged, block, far_send.at[step], far_receive.at[step])
        for step, other in enumerate(far)
    ]
    near = [remote("fsdp", sibling, staged, block, near_send.at[chips - 1], near_receive.at[chips - 1])]
    for step in range(1, chips):
        away[step - 1].wait_recv()
        origin = lax.rem(chip + chips - step, chips) * 2 + core
        arrived = target.at[:, origin]
        near.append(
            remote("fsdp", sibling, arrived, arrived, near_send.at[step - 1], near_receive.at[step - 1])
        )
    for copy in away:
        copy.wait_send()
    for copy in near:
        copy.wait()
    keep.wait()


def columns_of(weight, count, number):
    chips = count // 2
    dma = pltpu.SemaphoreType.DMA
    return call(
        functools.partial(columns_kernel, count),
        (weight,),
        jax.ShapeDtypeStruct((4, count, *weight.shape[1:]), weight.dtype),
        [
            pltpu.VMEM(weight.shape, weight.dtype),
            dma((3,)),
            dma((3,)),
            dma((2,)),
            dma((chips - 1,)),
            dma((chips - 1,)),
            dma((chips,)),
            dma((chips,)),
        ],
        number,
    )


def collect_kernel(source, target, mine, first, second_in, outgoing, load, send, receive, store):
    me = lax.axis_index("seq")
    one, two, both = me ^ 1, me ^ 2, me ^ 3
    width = source.shape[3] // 2
    greet("seq", [one, two])
    copies = []
    for side, (near, rest) in enumerate(((one, two), (two, one))):
        lanes = pl.ds(side * width, width)
        for order, block in enumerate((both, near)):
            copies.append(
                remote(
                    "seq",
                    near,
                    source.at[:, block, :, lanes],
                    first.at[side, order],
                    send.at[side, order],
                    receive.at[side, order],
                )
            )
        for order, block in enumerate((rest, me)):
            pltpu.make_async_copy(
                source.at[:, block, :, lanes], mine.at[side, order], load.at[side, order]
            ).start()
    passed = []
    for side, rest in enumerate((two, one)):
        copies[side * 2].wait_recv()
        pltpu.make_async_copy(mine.at[side, 0], mine.at[side, 0], load.at[side, 0]).wait()
        outgoing[side] = (
            mine[side, 0].astype(jnp.float32) + first[side, 0].astype(jnp.float32)
        ).astype(outgoing.dtype)
        passed.append(
            remote("seq", rest, outgoing.at[side], second_in.at[side], send.at[2, side], receive.at[2, side])
        )
    for side in range(2):
        copies[side * 2 + 1].wait_recv()
        pltpu.make_async_copy(mine.at[side, 1], mine.at[side, 1], load.at[side, 1]).wait()
        passed[side].wait_recv()
        mine[side, 1] = (
            mine[side, 1].astype(jnp.float32)
            + first[side, 1].astype(jnp.float32)
            + second_in[side].astype(jnp.float32)
        ).astype(mine.dtype)
        out = pltpu.make_async_copy(
            mine.at[side, 1], target.at[:, :, pl.ds(side * width, width)], store.at[side]
        )
        out.start()
    for side in range(2):
        pltpu.make_async_copy(
            mine.at[side, 1], target.at[:, :, pl.ds(side * width, width)], store.at[side]
        ).wait()
    for copy in copies + passed:
        copy.wait_send()


def collect(source, number):
    a, _, rows, width = source.shape
    dma = pltpu.SemaphoreType.DMA
    block = (a, rows, width // 2)
    return call(
        collect_kernel,
        (source,),
        jax.ShapeDtypeStruct((a, rows, width), source.dtype),
        [
            pltpu.VMEM((2, 2, *block), source.dtype),
            pltpu.VMEM((2, 2, *block), source.dtype),
            pltpu.VMEM((2, *block), source.dtype),
            pltpu.VMEM((2, *block), source.dtype),
            dma((2, 2)),
            dma((3, 2)),
            dma((3, 2)),
            dma((2,)),
        ],
        number,
    )


def masked_scores(block_query, keys, start, length, scale):
    scores = (
        jnp.einsum("qhd,khd->hqk", block_query, keys, preferred_element_type=jnp.float32) * scale
    )
    rows = start + jnp.arange(block_query.shape[0], dtype=jnp.int32)
    columns = jnp.arange(keys.shape[0], dtype=jnp.int32)
    keep = (columns[None, :] <= rows[:, None]) & (columns[None, :] < length)
    return jnp.where(keep[None], scores, MASKED)


def shards(
    hidden,
    lengths,
    expert_ids,
    attn_gain,
    qkv_weight,
    out_weight,
    moe_gain,
    router_weight,
    expert_in,
    expert_out,
    out_grad,
):
    S = jax.ShapeDtypeStruct
    low = jnp.bfloat16
    owners = lax.axis_size("fsdp")
    seq_place = lax.axis_index("seq")
    seq_count = lax.axis_size("seq")
    tokens, width = hidden.shape[1], hidden.shape[2]
    full_len = tokens * seq_count
    group_width = width // seq_count
    heads_local = group_width // HEAD_DIM
    rows_own = qkv_weight.shape[0]
    scale = HEAD_DIM ** (-0.5)
    length = lengths[0]
    experts_all = router_weight.shape[1]
    small = jnp.concatenate([router_weight, attn_gain[:, None], moe_gain[:, None]], axis=1)
    small = jnp.pad(small, ((0, 0), (0, -small.shape[1] % 128)))
    small = lax.all_gather(small, ("seq", "fsdp"), axis=0, tiled=True)
    weight_mix = lax.all_gather(out_weight, ("seq", "fsdp"), axis=0, tiled=True)
    weight_route = small[:, :experts_all]
    gain_one = small[:, experts_all].astype(jnp.float32)
    gain_two = small[:, experts_all + 1].astype(jnp.float32)
    mix_rows = lax.dynamic_slice_in_dim(weight_mix, seq_place * group_width, group_width, 0)

    expert_local = expert_in.shape[0]
    capacity = -(-max(2, 2 * tokens // experts_all) // 16) * 16
    slots = experts_all * capacity

    position = seq_place * tokens + jnp.arange(tokens, dtype=jnp.int32)
    valid = (position < length).astype(jnp.float32)[:, None]
    chosen = expert_ids[0, :, 0]
    choose = chosen[:, None] == jnp.arange(experts_all, dtype=jnp.int32)[None, :]
    order = jnp.arange(tokens, dtype=jnp.int32)
    earlier = (order[None, :] < order[:, None]) & (chosen[None, :] == chosen[:, None])
    ranks = jnp.sum(earlier.astype(jnp.int32), axis=1)
    slot = chosen * capacity + ranks
    hit = jnp.arange(slots, dtype=jnp.int32)[:, None] == slot[None, :]
    dispatch = hit.astype(low)

    def to_owners(rows, number):
        return exchange(
            "fsdp",
            owners,
            (rows.reshape(owners, expert_local, capacity, width),),
            (S((expert_local, owners, capacity, width), low),),
            ((lead, second),),
            number,
        )[0].reshape(expert_local, owners * capacity, width)

    def to_sources(rows, number):
        return exchange(
            "fsdp",
            owners,
            (rows.reshape(expert_local, owners, capacity, width),),
            (S((owners, expert_local, capacity, width), low),),
            ((second, lead),),
            number,
        )[0].reshape(slots, width)

    upstream_low = jnp.where(valid > 0, out_grad[0], 0).astype(low)
    upstream = upstream_low.astype(jnp.float32)
    up_rows = times(dispatch, upstream_low).astype(low)
    up_all = spread(to_owners(up_rows, 0), 1)

    weight_qkv = columns_of(
        qkv_weight.reshape(rows_own, 3, seq_count, group_width)
        .transpose(2, 0, 1, 3)
        .reshape(seq_count, rows_own, 3 * group_width),
        owners,
        2,
    ).reshape(width, 3 * group_width)
    hidden_all = spread(hidden, 3).reshape(full_len, width)

    normed = scaled_norm(hidden_all.astype(jnp.float32), gain_one).astype(low)
    projected = times(normed, weight_qkv).astype(low)
    query = projected[:, :group_width].reshape(full_len, heads_local, HEAD_DIM)
    keys = projected[:, group_width : 2 * group_width].reshape(full_len, heads_local, HEAD_DIM)
    values = projected[:, 2 * group_width :].reshape(full_len, heads_local, HEAD_DIM)
    starts = list(range(0, full_len, QBLOCK))
    outputs = []
    totals = []
    for start in starts:
        block_query = query[start : start + QBLOCK]
        reach = start + QBLOCK
        scores = masked_scores(block_query, keys[:reach], start, length, scale)
        top = jnp.max(scores, axis=-1, keepdims=True)
        total = top + jnp.log(jnp.sum(jnp.exp(scores - top), axis=-1, keepdims=True))
        probs = jnp.exp(scores - total).astype(low)
        block_out = jnp.einsum("hqk,khd->qhd", probs, values[:reach], preferred_element_type=jnp.float32)
        outputs.append(block_out.astype(low))
        totals.append(total)
    attended = jnp.concatenate(outputs, axis=0).reshape(full_len, group_width)
    mixed = exchange(
        "seq",
        seq_count,
        (attended.reshape(seq_count, tokens, group_width),),
        (S((seq_count, tokens, group_width), low),),
        ((lead, lead),),
        4,
    )[0]
    mixed = mixed.transpose(1, 0, 2).reshape(tokens, width)
    inputs = hidden[0].astype(jnp.float32)
    middle = inputs + times(mixed, weight_mix)
    normed_two, norm_two_back = jax.vjp(scaled_norm, middle, gain_two)
    normed_two = normed_two.astype(low)
    logits = times(normed_two, weight_route)

    def gate_of(logit_rows):
        return jnp.sum(jnp.where(choose, jax.nn.softmax(logit_rows, axis=-1), 0.0), axis=-1)

    gate, gate_back = jax.vjp(gate_of, logits)
    gate_rows = jnp.sum(jnp.where(hit, gate[None, :], 0.0), axis=1)
    gates = lax.all_to_all(
        gate_rows.reshape(owners, expert_local, capacity), "fsdp", split_axis=0, concat_axis=0, tiled=True
    )
    gates = lax.all_gather(gates, "seq", axis=0)
    gates = gates.transpose(2, 0, 1, 3).reshape(expert_local, seq_count * owners * capacity, 1)

    sent = times(dispatch, normed_two).astype(low)
    rows_all = spread(to_owners(sent, 5), 6)
    count = seq_count * owners * capacity
    rows_all = rows_all.reshape(expert_local, count, width)
    up_all = up_all.reshape(expert_local, count, width)
    grad_rows = (up_all.astype(jnp.float32) * gates).astype(low)

    def per_expert(form, left, right):
        return jnp.einsum(form, left, right, preferred_element_type=jnp.float32)

    inner = per_expert("jrd,jdf->jrf", rows_all, expert_in)
    active, active_back = jax.vjp(gelu_tanh, inner)
    active = active.astype(low)
    partial_out = per_expert("jrf,jfd->jrd", active, expert_out).astype(low)
    grad_active = per_expert("jrd,jfd->jrf", grad_rows, expert_out)
    grad_inner = active_back(grad_active)[0].astype(low)
    partial_back = per_expert("jrf,jdf->jrd", grad_inner, expert_in).astype(low)
    expert_out_grad = per_expert("jrf,jrd->jfd", active, grad_rows)
    expert_in_grad = per_expert("jrd,jrf->jdf", rows_all, grad_inner)

    shape = (expert_local, seq_count, owners * capacity, width)
    returned = to_sources(collect(partial_out.reshape(shape), 7), 8)
    grad_back = to_sources(collect(partial_back.reshape(shape), 9), 10)

    back_rows = transposed_times(dispatch, returned)
    output = valid * (middle + gate[:, None] * back_rows)
    grad_gate = jnp.sum(upstream * back_rows, axis=1)
    grad_logits = gate_back(grad_gate)[0].astype(low)
    grad_route = transposed_times(normed_two, grad_logits)
    grad_normed_two = times_transposed(grad_logits, weight_route) + transposed_times(dispatch, grad_back)
    grad_middle, grad_gain_two = norm_two_back(grad_normed_two)
    grad_middle = grad_middle + upstream
    grad_attn = grad_middle.astype(low)

    grad_attn_all = spread(grad_attn[None], 11).reshape(full_len, width)
    grad_mix = transposed_times(attended, grad_attn_all)
    grad_heads = times_transposed(grad_attn_all, mix_rows).astype(low)
    grad_heads = grad_heads.reshape(full_len, heads_local, HEAD_DIM)
    grad_query = []
    grad_keys = jnp.zeros((full_len, heads_local, HEAD_DIM), jnp.float32)
    grad_values = jnp.zeros((full_len, heads_local, HEAD_DIM), jnp.float32)
    for number, start in enumerate(starts):
        reach = start + QBLOCK
        block_query = query[start : start + QBLOCK]
        scores = masked_scores(block_query, keys[:reach], start, length, scale)
        probs = jnp.exp(scores - totals[number])
        probs_low = probs.astype(low)
        grad_out = grad_heads[start : start + QBLOCK]
        grad_values = grad_values.at[:reach].add(
            jnp.einsum("hqk,qhd->khd", probs_low, grad_out, preferred_element_type=jnp.float32)
        )
        grad_probs = jnp.einsum(
            "qhd,khd->hqk", grad_out, values[:reach], preferred_element_type=jnp.float32
        )
        grad_scores = (
            probs * (grad_probs - jnp.sum(grad_probs * probs, axis=-1, keepdims=True))
        ).astype(low)
        grad_query.append(
            jnp.einsum("hqk,khd->qhd", grad_scores, keys[:reach], preferred_element_type=jnp.float32)
            * scale
        )
        grad_keys = grad_keys.at[:reach].add(
            jnp.einsum("hqk,qhd->khd", grad_scores, block_query, preferred_element_type=jnp.float32)
            * scale
        )
    grad_projected = jnp.concatenate(
        [
            part.astype(low).reshape(full_len, group_width)
            for part in (jnp.concatenate(grad_query, axis=0), grad_keys, grad_values)
        ],
        axis=1,
    )
    grad_qkv_cols = transposed_times(normed, grad_projected).astype(low)
    partial_normed = times_transposed(grad_projected, weight_qkv).astype(low)
    grad_normed = collect(partial_normed.reshape(1, seq_count, tokens, width), 12)[0]

    qkv_parts, mix_parts = exchange(
        "fsdp",
        owners,
        (
            grad_qkv_cols.reshape(seq_count, owners, rows_own, 3 * group_width),
            grad_mix.astype(low).reshape(owners, rows_own, width),
        ),
        (
            S((owners, seq_count, rows_own, 3 * group_width), low),
            S((owners, rows_own, width), low),
        ),
        ((second, lead), (lead, lead)),
        13,
    )
    mix_grad = jnp.sum(mix_parts.astype(jnp.float32), axis=0)
    qkv_sum = jnp.sum(qkv_parts.astype(jnp.float32), axis=0)
    qkv_sum = exchange(
        "seq", seq_count, (qkv_sum,), (S(qkv_sum.shape, jnp.float32),), ((lead, lead),), 14
    )[0]
    qkv_weight_grad = (
        qkv_sum.reshape(seq_count, rows_own, 3, group_width)
        .transpose(1, 2, 0, 3)
        .reshape(rows_own, 3 * width)
    )
    _, norm_back = jax.vjp(scaled_norm, inputs, gain_one)
    grad_inputs, grad_gain_one = norm_back(grad_normed.astype(jnp.float32))
    grad_inputs = grad_inputs + grad_middle
    small_grad = jnp.concatenate(
        [grad_route, grad_gain_one[:, None], grad_gain_two[:, None]], axis=1
    )
    small_grad = jnp.pad(small_grad, ((0, 0), (0, -small_grad.shape[1] % 128)))
    small_grad = lax.psum_scatter(small_grad, ("seq", "fsdp"), scatter_dimension=0, tiled=True)
    return (
        output.astype(low)[None],
        grad_inputs[None],
        small_grad[:, experts_all],
        qkv_weight_grad,
        mix_grad,
        small_grad[:, experts_all + 1],
        small_grad[:, :experts_all],
        expert_in_grad,
        expert_out_grad,
    )


def solution(mesh):
    placed = (
        P("fsdp", "seq", None),
        P("fsdp"),
        P("fsdp", "seq", None),
        P(("seq", "fsdp")),
        P(("seq", "fsdp"), None),
        P(("seq", "fsdp"), None),
        P(("seq", "fsdp")),
        P(("seq", "fsdp"), None),
        P("fsdp", None, "seq"),
        P("fsdp", "seq", None),
        P("fsdp", "seq", None),
    )
    return jax.shard_map(
        shards,
        mesh=mesh,
        in_specs=placed,
        out_specs=(
            P("fsdp", "seq", None),
            P("fsdp", "seq", None),
            P(("seq", "fsdp")),
            P(("seq", "fsdp"), None),
            P(("seq", "fsdp"), None),
            P(("seq", "fsdp")),
            P(("seq", "fsdp"), None),
            P("fsdp", None, "seq"),
            P("fsdp", "seq", None),
        ),
        check_vma=False,
    )
```

time: 1120 us -> 732 us (0.65)
  waiting for transfers between devices: 634 us -> 128 us
  Pallas kernels: 0 us -> 379 us
  blocking collectives: 224 us -> 52.3 us
  matrix products: 133 us -> 96.3 us
  local copies, waits for them, and re-layouts: 53.2 us -> 18.7 us
  other arithmetic: 34.8 us -> 22 us
  starting transfers between devices: 22.3 us -> 9.75 us
    reduce_scatter x4 -> x0, waiting for transfers between devices: 407 us -> none  [the longest x2 173 us: collect_rows(): return lax.psum_scatter(value, 'seq', scatter_dimension=2, tiled=True)]
    pallas_call x0 -> x15, Pallas kernels: none -> 379 us  [call(): pl.pallas_call(kernel, out_shape=outputs, in_specs=[ANY] * len(inputs), o...]
    all_gather x4 -> x1, waiting for transfers between devices: 135 us -> 0.01 us  [shards(): weight_mix = lax.all_gather(out_weight, ('seq', 'fsdp'), axis=0, tiled=True)]
    unnamed x10 -> x3, waiting for transfers between devices: 30.3 us -> 123 us
    all_to_all x3 -> x0, blocking collectives: 86.6 us -> none  [the longest x2 59 us: to_owners(): lax.all_to_all(value, 'fsdp', split_axis=0, concat_axis=0, tiled=True)]
    unnamed x2 -> x0, blocking collectives: 80.7 us -> none
    all_to_all x5 -> x1, waiting for transfers between devices: 61.9 us -> 4.39 us  [shards(): lax.all_to_all(gate_rows.reshape(owners, expert_local, capacity), 'fsdp',...]
    dot_general x19 -> x17, matrix products: 96.8 us -> 77.5 us  [the longest x6 60.1 us: per_expert(): return jnp.einsum(form, left, right, preferred_element_type=jnp.float32)]
  transfers between devices with their start and end apart: 14 -> 3, of which waited for: 13 -> 2; matrix products, arithmetic and copies ran while one was open for 12% -> 6% of each run, Pallas kernels for 0% -> 17%
where the time goes in v2:
time: 732 us; the launch traced here: 722 us
  Pallas kernels  379 us (52%)
  waiting for transfers between devices  128 us (17%)
  matrix products  96.3 us (13%)
  blocking collectives  52.3 us (7%)
  other arithmetic  22 us (3%)
  local copies, waits for them, and re-layouts  18.7 us (3%)
  between operations  15.8 us (2%)
  starting transfers between devices  9.75 us (1%)
    pallas_call x15, Pallas kernels, call(): pl.pallas_call(kernel, out_shape=outputs, in_specs=[ANY] * len(inputs), o...  379 us
    unnamed x3, waiting for transfers between devices  123 us
    dot_general x6, matrix products, per_expert(): return jnp.einsum(form, left, right, preferred_element_type=jnp.float32)  60.1 us
    all_gather x1, blocking collectives, shards(): small = lax.all_gather(small, ('seq', 'fsdp'), axis=0, tiled=True)  44.5 us
  transfers between devices with their start and end apart: 3, of which 2 were waited for; matrix products, arithmetic and copies ran while one was open for 6% of the time, Pallas kernels for 17%

profile of v2, /device:TPU:0, one launch (start us, length us, event | category | flops | bytes accessed | tf_op | source)
XLA Modules:
  0.0 721.8 jit_solution(1874129511450670399)
XLA Ops:
  8.6 0.9 convert_reduce_fusion.4
  12.5 1.1 reshape.461
  14.0 44.5 %all_gather.12 = bf16[1024,128]{1,0:T(8,128)(2,1)S(1)} all-gather(bf16[32,128]{1,0:T(8,128)(2,1)S(1)} %fusion.55), channel_id=1, replica_groups=mesh['seq'=4,'fsdp'=8] {'seq','fsdp'}, dimensions={0}, use_global_device_ids=true | all-gather | bytes 270336 | tf_op jit(solution)/shard_map/all_gather | solution.py:353
  59.0 1.7 convolution_convert_fusion.5
  60.7 20.7 %shard_map.195 = bf16[2,8,32,1024]{3,2,1,0:T(8,128)(2,1)S(1)} custom-call(bf16[8,2,32,1024]{3,2,1,0:T(8,128)(2,1)S(1)} %bitcast.181), custom_call_target="tpu_custom_call" | custom-call | tf_op jit(solution)/shard_map/pallas_call | solution.py:58
  81.4 28.5 %shard_map.189 = bf16[4,8,32,768]{3,2,1,0:T(8,128)(2,1)S(1)} custom-call(bf16[4,32,768]{2,1,0:T(8,128)(2,1)S(1)} %reshape.462.source), custom_call_target="tpu_custom_call" | custom-call | tf_op jit(solution)/shard_map/pallas_call | solution.py:58
  109.9 21.1 %shard_map.188 = bf16[1,4,256,1024]{3,2,1,0:T(8,128)(2,1)S(1)} custom-call(bf16[1,256,1024]{2,1,0:T(8,128)(2,1)S(1)} %copy-done.1), custom_call_target="tpu_custom_call" | custom-call | tf_op jit(solution)/shard_map/pallas_call | solution.py:58
  132.0 1.8 convolution_convert_fusion.4
  134.0 36.1 %shard_map.196 = bf16[2,4,256,1024]{3,2,1,0:T(8,128)(2,1)S(1)} custom-call(bf16[2,256,1024]{2,1,0:T(8,128)(2,1)S(1)} %bitcast.167), custom_call_target="tpu_custom_call" | custom-call | tf_op jit(solution)/shard_map/pallas_call | solution.py:58
  170.1 0.9 fusion.12
  171.1 0.9 exponential_reduce_fusion.1
  172.7 1.7 fusion.8
  174.4 2.4 exponential_reduce_fusion
  176.9 1.2 fusion.25
  178.1 2.4 fusion.24
  180.5 0.8 copy-done.28
  181.3 1.2 reshape_reshape.3
  182.5 1.3 copy.82.refs_0_
  183.8 7.4 %shard_map.190 = bf16[4,256,256]{2,1,0:T(8,128)(2,1)S(1)} custom-call(bf16[4,256,256]{2,1,0:T(8,128)(2,1)S(1)} %copy.82.refs_0_), custom_call_target="tpu_custom_call" | custom-call | tf_op jit(solution)/shard_map/pallas_call | solution.py:58
  192.0 1.2 copy.83
  194.0 1.9 fusion.11
  195.9 2.4 multiply_reduce_fusion.5
  199.3 23.7 %shard_map.191 = bf16[2,8,32,1024]{3,2,1,0:T(8,128)(2,1)S(1)} custom-call(bf16[8,2,32,1024]{3,2,1,0:T(8,128)(2,1)S(1)} %bitcast.171), custom_call_target="tpu_custom_call" | custom-call | tf_op jit(solution)/shard_map/pallas_call | solution.py:58
  223.0 37.7 %shard_map.192 = bf16[2,4,256,1024]{3,2,1,0:T(8,128)(2,1)S(1)} custom-call(bf16[2,256,1024]{2,1,0:T(8,128)(2,1)S(1)} %bitcast.168), custom_call_target="tpu_custom_call" | custom-call | tf_op jit(solution)/shard_map/pallas_call | solution.py:58
  260.7 10.4 %fusion.75 = f32[2,1024,1024]{2,1,0:T(8,128)} fusion(bf16[2,1024,1024]{2,1,0:T(8,128)(2,1)S(1)} %bitcast.163, bf16[2,1024,1024]{2,1,0:T(8,128)(2,1)} %param.31), kind=kOutput, calls=%fused_computation.157 | convolution fusion | flops 4294967296 | bytes 16777216 | tf_op jit(solution)/shard_map/jrd,jdf->jrf/dot_general | solution.py:462
  271.1 8.5 %convolution_convert_fusion.1 = bf16[2,1024,1024]{2,1,0:T(8,128)(2,1)S(1)} fusion(bf16[2,1024,1024]{2,1,0:T(8,128)(2,1)S(1)} %copy-done.36, f32[2,1024,1024]{2,1,0:T(8,128)} %fusion.75), kind=kOutput, calls=%fused_computation.32 | convolution fusion | flops 4315938816 | bytes 16777216 | tf_op jit(solution)/shard_map/jrf,jfd->jrd/dot_general | solution.py:462
  279.6 37.3 %shard_map.193 = bf16[2,256,1024]{2,1,0:T(8,128)(2,1)S(1)} custom-call(bf16[2,4,256,1024]{3,2,1,0:T(8,128)(2,1)S(1)} %bitcast.165), custom_call_target="tpu_custom_call" | custom-call | tf_op jit(solution)/shard_map/pallas_call | solution.py:58
  317.0 23.9 %shard_map.194 = bf16[8,2,32,1024]{3,2,1,0:T(8,128)(2,1)S(1)} custom-call(bf16[2,8,32,1024]{3,2,1,0:T(8,128)(2,1)S(1)} %bitcast.169), custom_call_target="tpu_custom_call" | custom-call | tf_op jit(solution)/shard_map/pallas_call | solution.py:58
  340.9 1.5 fusion.26
  343.2 9.7 %all-to-all-start = ((f32[8,2,32]{2,1,0:T(2,128)}), f32[8,2,32]{2,1,0:T(2,128)S(1)}, u32[]{:S(2)}, u32[]{:S(2)}) async-start(f32[8,2,32]{2,1,0:T(2,128)} %reshape.475), calls=%async_computation | async-start | bytes 16384 | tf_op jit(solution)/shard_map/all_to_all | solution.py:448
  353.3 0.8 fusion.62
  354.1 4.4 all-to-all-done
  358.5 7.8 %all-gather = f32[32,2,32]{2,1,0:T(2,128)S(1)} all-gather(f32[8,2,32]{2,1,0:T(2,128)S(1)} %all-to-all-done), channel_id=2, replica_groups=mesh['seq'=4,'fsdp'=8] {'seq'}, dimensions={0}, use_global_device_ids=true | all-gather | bytes 10240 | tf_op jit(solution)/shard_map/all_gather | solution.py:451
  366.4 3.1 fusion.7
  369.9 11.3 %fusion.6 = bf16[2,1024,1024]{2,1,0:T(8,128)(2,1)S(1)} fusion(f32[2,1024,1024]{2,1,0:T(8,128)} %fusion.75, bf16[2,1024,1024]{2,1,0:T(8,128)(2,1)S(1)} %fusion.7, bf16[2,1024,1024]{2,1,0:T(8,128)(2,1)S(1)} %copy-done.37), kind=kOutput, calls=%fused_computation.8 | convolution fusion | flops 4336910336 | bytes 20971520 | tf_op jit(solution)/shard_map/jrd,jfd->jrf/dot_general | solution.py:462
  381.2 13.7 %fusion.69 = f32[2,1024,1024]{2,1,0:T(8,128)} fusion(bf16[2,1024,1024]{2,1,0:T(8,128)(2,1)S(1)} %fusion.7, f32[2,1024,1024]{2,1,0:T(8,128)} %fusion.75), kind=kOutput, calls=%fused_computation.151 | convolution fusion | flops 4313841664 | bytes 20971520 | tf_op jit(solution)/shard_map/jrf,jrd->jfd/dot_general | solution.py:462
  394.9 4.8 convolution_convert_fusion
  399.7 35.0 %shard_map.197 = bf16[2,256,1024]{2,1,0:T(8,128)(2,1)S(1)} custom-call(bf16[2,4,256,1024]{3,2,1,0:T(8,128)(2,1)S(1)} %bitcast.166), custom_call_target="tpu_custom_call" | custom-call | tf_op jit(solution)/shard_map/pallas_call | solution.py:58
  434.7 18.7 %shard_map.198 = bf16[8,2,32,1024]{3,2,1,0:T(8,128)(2,1)S(1)} custom-call(bf16[2,8,32,1024]{3,2,1,0:T(8,128)(2,1)S(1)} %bitcast.170), custom_call_target="tpu_custom_call" | custom-call | tf_op jit(solution)/shard_map/pallas_call | solution.py:58
  454.1 1.3 convert_bitcast_fusion
  455.5 18.9 %shard_map.199 = bf16[1,4,256,1024]{3,2,1,0:T(8,128)(2,1)S(1)} custom-call(bf16[1,256,1024]{2,1,0:T(8,128)(2,1)S(1)} %get-tuple-element.85.source), custom_call_target="tpu_custom_call" | custom-call | tf_op jit(solution)/shard_map/pallas_call | solution.py:58
  474.3 1.8 convolution_convert_fusion.8
  476.2 2.0 convolution_bitcast_fusion.1
  478.2 1.5 multiply_reduce_fusion.1
  480.4 1.3 multiply_convert_fusion.2
  481.7 1.2 fusion.22
  484.4 3.1 multiply_reduce_fusion
  487.6 3.1 fusion.19
  490.7 2.8 multiply_convert_fusion
  493.5 1.4 fusion.23
  494.9 0.9 fusion.18
  496.5 1.8 convolution_convert_fusion.2
  498.4 1.9 convolution_convert_fusion.3
  500.2 20.4 %shard_map.200 = bf16[1,256,1024]{2,1,0:T(8,128)(2,1)S(1)} custom-call(bf16[1,4,256,1024]{3,2,1,0:T(8,128)(2,1)S(1)} %bitcast.176), custom_call_target="tpu_custom_call" | custom-call | tf_op jit(solution)/shard_map/pallas_call | solution.py:58
  520.6 42.6 %shard_map.201 = (bf16[8,4,32,768]{3,2,1,0:T(8,128)(2,1)S(1)}, bf16[8,32,1024]{2,1,0:T(8,128)(2,1)S(1)}) custom-call(bf16[4,8,32,768]{3,2,1,0:T(8,128)(2,1)S(1)} %bitcast.180, bf16[8,32,1024]{2,1,0:T(8,128)(2,1)S(1)} %bitcast.182), custom_call_target="tpu_custom_call" | custom-call | tf_op jit(solution)/shard_map/pallas_call | solution.py:58
  564.7 1.1 copy.102
  565.8 0.8 pad.21.clone
  566.7 1.3 fusion.29
  568.7 7.3 %shard_map.202 = f32[4,32,768]{2,1,0:T(8,128)S(1)} custom-call(f32[4,32,768]{2,1,0:T(8,128)S(1)} %convert_reduce_fusion.refs_0_), custom_call_target="tpu_custom_call" | custom-call | tf_op jit(solution)/shard_map/pallas_call | solution.py:58
  576.5 0.9 reshape.487
  577.4 11.4 %fusion.76 = f32[2,1024,1024]{2,1,0:T(8,128)} fusion(bf16[2,1024,1024]{2,1,0:T(8,128)(2,1)} %bitcast.164, bf16[2,1024,1024]{2,1,0:T(8,128)(2,1)} %copy-done.41), kind=kOutput, calls=%fused_computation.158 | convolution fusion | flops 4294967296 | bytes 16777216 | tf_op jit(solution)/shard_map/jrd,jrf->jdf/dot_general | solution.py:462
  588.8 122.5 %reduce-scatter.4.cloned.1.call-done = f32[32,128]{1,0:T(8,128)} async-done(((f32[1024,128]{1,0:T(8,128)}), f32[32,128]{1,0:T(8,128)}) %reduce-scatter.4.cloned.1.call-update) | async-done | bytes 16400
  711.3 1.4 copy.101
  712.7 0.9 fusion.73
  (145 shorter events, 18.1 us)
Async XLA Ops:
  7.2 102.7 %copy-start.1 = (bf16[1,256,1024]{2,1,0:T(8,128)(2,1)S(1)}, bf16[1,256,1024]{2,1,0:T(8,128)(2,1)}, u32[]{:S(2)}) copy-start(bf16[1,256,1024]{2,1,0:T(8,128)(2,1)} %source.1) | copy-start | bytes 1572868
  7.2 188.7 %all-gather.3.cloned.1.call-start = ((), (), s32[]{:S(2)}) async-start(), calls=%async_computation.2 | async-start | bytes 2162688 | tf_op jit(solution)/shard_map/all_gather | solution.py:354
  59.0 117.8 %copy-start.12 = (pred[512,512]{0,1:T(8,128)(4,1)}, pred[512,512]{0,1:T(8,128)(4,1)S(1)}, u32[]{:S(2)}) copy-start(pred[512,512]{0,1:T(8,128)(4,1)S(1)} %fusion.32) | copy-start | bytes 786436
  109.9 22.2 %copy-start.4 = (bf16[4,8,32,768]{3,2,1,0:T(8,128)(2,1)}, bf16[4,8,32,768]{3,2,1,0:T(8,128)(2,1)S(1)}, u32[]{:S(2)}) copy-start(bf16[4,8,32,768]{3,2,1,0:T(8,128)(2,1)S(1)} %shard_map.189) | copy-start | bytes 4718596
  134.0 37.1 %copy-start.19 = (bf16[512,256]{0,1:T(8,128)(2,1)}, bf16[512,256]{0,1:T(8,128)(2,1)S(1)}, u32[]{:S(2)}) copy-start(bf16[512,256]{0,1:T(8,128)(2,1)S(1)} %get-tuple-element.87) | copy-start | bytes 786436
  134.0 37.1 %copy-start.21 = (bf16[512,256]{0,1:T(8,128)(2,1)}, bf16[512,256]{0,1:T(8,128)(2,1)S(1)}, u32[]{:S(2)}) copy-start(bf16[512,256]{0,1:T(8,128)(2,1)S(1)} %get-tuple-element.89) | copy-start | bytes 786436
  134.0 38.7 %copy-start.17 = (bf16[512,256]{0,1:T(8,128)(2,1)}, bf16[512,256]{0,1:T(8,128)(2,1)S(1)}, u32[]{:S(2)}) copy-start(bf16[512,256]{0,1:T(8,128)(2,1)S(1)} %get-tuple-element.88) | copy-start | bytes 786436
  134.0 42.9 %copy-start.30 = (bf16[512,256]{0,1:T(8,128)(2,1)}, bf16[512,256]{0,1:T(8,128)(2,1)S(1)}, u32[]{:S(2)}) copy-start(bf16[512,256]{0,1:T(8,128)(2,1)S(1)} %get-tuple-element.90) | copy-start | bytes 786436
  170.1 2.0 copy-start
  171.1 5.8 copy-start.7
  172.6 5.5 copy-start.10
  172.7 1.7 copy-start.14
  172.7 5.4 copy-start.26
  174.4 3.7 copy-start.6
  180.5 0.8 copy-start.28
  191.2 0.8 copy-start.3
  260.7 10.5 %copy-start.2 = (bf16[2,4,256,1024]{3,2,1,0:T(8,128)(2,1)}, bf16[2,4,256,1024]{3,2,1,0:T(8,128)(2,1)S(1)}, u32[]{:S(2)}) copy-start(bf16[2,4,256,1024]{3,2,1,0:T(8,128)(2,1)S(1)} %shard_map.192) | copy-start | bytes 12582916
  260.7 10.5 %copy-start.36 = (bf16[2,1024,1024]{2,1,0:T(8,128)(2,1)S(1)}, bf16[2,1024,1024]{2,1,0:T(8,128)(2,1)}, u32[]{:S(2)}) copy-start(bf16[2,1024,1024]{2,1,0:T(8,128)(2,1)} %param.32) | copy-start | bytes 12582916
  279.6 61.3 %copy-start.23 = (bf16[1,256,1024]{2,1,0:T(8,128)(2,1)S(1)}, bf16[1,256,1024]{2,1,0:T(8,128)(2,1)}, u32[]{:S(2)}) copy-start(bf16[1,256,1024]{2,1,0:T(8,128)(2,1)} %param.33) | copy-start | bytes 1572868
  279.6 62.7 %copy-start.34 = (s32[1,256,1]{1,2,0:T(1,128)S(1)}, s32[1,256,1]{1,2,0:T(1,128)}, u32[]{:S(2)}) copy-start(s32[1,256,1]{1,2,0:T(1,128)} %param.25) | copy-start | bytes 3076
  343.2 15.3 %all-to-all-start = ((f32[8,2,32]{2,1,0:T(2,128)}), f32[8,2,32]{2,1,0:T(2,128)S(1)}, u32[]{:S(2)}, u32[]{:S(2)}) async-start(f32[8,2,32]{2,1,0:T(2,128)} %reshape.475), calls=%async_computation | async-start | bytes 16384 | tf_op jit(solution)/shard_map/all_to_all | solution.py:448
  352.9 358.4 %reduce-scatter.4.cloned.1.call-start = ((), (), s32[]{:S(2)}) async-start(), calls=%async_computation.3 | async-start | bytes 540672
  366.4 3.5 copy-start.37
  381.2 13.8 %copy-start.41 = (bf16[2,1024,1024]{2,1,0:T(8,128)(2,1)}, bf16[2,1024,1024]{2,1,0:T(8,128)(2,1)S(1)}, u32[]{:S(2)}) copy-start(bf16[2,1024,1024]{2,1,0:T(8,128)(2,1)S(1)} %fusion.6) | copy-start | bytes 12582916
  381.2 13.7 %copy-start.38 = (bf16[2,1024,1024]{2,1,0:T(8,128)(2,1)S(1)}, bf16[2,1024,1024]{2,1,0:T(8,128)(2,1)}, u32[]{:S(2)}) copy-start(bf16[2,1024,1024]{2,1,0:T(8,128)(2,1)} %param.31) | copy-start | bytes 12582916
  434.7 19.4 %copy-start.16 = (f32[256,1024]{1,0:T(8,128)S(1)}, f32[256,1024]{1,0:T(8,128)}, u32[]{:S(2)}) copy-start(f32[256,1024]{1,0:T(8,128)} %get-tuple-element.109) | copy-start | bytes 3145732
  434.7 19.4 %copy-start.24 = (bf16[1,256,1024]{2,1,0:T(8,128)(2,1)S(1)}, bf16[1,256,1024]{2,1,0:T(8,128)(2,1)}, u32[]{:S(2)}) copy-start(bf16[1,256,1024]{2,1,0:T(8,128)(2,1)} %param.33) | copy-start | bytes 1572868
  455.5 20.7 %copy-start.8 = (f32[4,512,512]{1,2,0:T(8,128)S(1)}, f32[4,512,512]{1,2,0:T(8,128)}, u32[]{:S(2)}) copy-start(f32[4,512,512]{1,2,0:T(8,128)} %copy-done.7) | copy-start | bytes 12582916
  455.5 20.7 %copy-start.13 = (pred[512,512]{0,1:T(8,128)(4,1)S(1)}, pred[512,512]{0,1:T(8,128)(4,1)}, u32[]{:S(2)}) copy-start(pred[512,512]{0,1:T(8,128)(4,1)} %copy-done.12) | copy-start | bytes 786436
  476.1 2.1 copy-start.31
  478.2 2.2 copy-start.9
  479.7 4.6 slice-start
  480.4 1.3 copy-start.20
  480.4 2.5 copy-start.22
  480.4 4.0 slice-start.1
  481.7 2.0 copy-start.29
  481.7 2.7 copy-start.11
  481.7 2.7 copy-start.27
  484.4 3.2 copy-start.40
  490.7 2.8 copy-start.15
  493.5 1.4 copy-start.18
  494.9 1.4 copy-start.5
  494.9 1.4 copy-start.32
  494.9 1.6 copy-start.39
  496.5 1.9 copy-start.25
  500.2 63.3 %copy-start.35 = (f32[256]{0:T(256)S(1)}, f32[256]{0:T(256)}, u32[]{:S(2)}) copy-start(f32[256]{0:T(256)} %fusion.57) | copy-start | bytes 3076
  500.2 63.8 %copy-start.33 = (f32[1024,16]{0,1:T(8,128)S(1)}, f32[1024,16]{0,1:T(8,128)}, u32[]{:S(2)}) copy-start(f32[1024,16]{0,1:T(8,128)} %fusion.62) | copy-start | bytes 196612
Sparse Core Ops, SparseCore 0:
  11.0 70.1 all-gather.2
  566.8 144.4 reduce-scatter.3

commit v3 on v2

--- a/solution.py
+++ b/solution.py
@@ -11,6 +11,9 @@
 QBLOCK = 512
 EPS = 1e-05
 MASKED = -1e30
+ROOT = 0.7978845608028654
+TILE = 256
+GRAD = 256
 MESH = pl.DeviceIdType.MESH
 ANY = pl.BlockSpec(memory_space=pl.ANY)
 
@@ -310,6 +313,304 @@
         ],
         number,
     )
+
+
+def moe_kernel(
+    chips, cap, experts_all, send_rows, up_rows, route, w_in, w_out,
+    ret, dw_in, dw_out,
+    R, U, G, A, I, PB, first, second, W1, W2, RT, stage,
+    load, own, z_send, z_recv, s_send, s_recv, y_send, y_recv,
+    c_send, c_recv, d_send, d_recv, r_send, r_recv, store,
+):
+    me, place = lax.axis_index("seq"), lax.axis_index("fsdp")
+    one, two, both = me ^ 1, me ^ 2, me ^ 3
+    chip, core = place // 2, lax.rem(place, 2)
+    sibling = place ^ 1
+    count = chips * 2
+    part = 2 * cap
+    chunk = 4 * part
+    barrier = pltpu.get_barrier_semaphore()
+    for peer in (one, two):
+        pl.semaphore_signal(barrier, inc=1, device_id={"seq": peer}, device_id_type=MESH)
+    for step in range(1, count):
+        pl.semaphore_signal(
+            barrier, inc=1, device_id={"fsdp": lax.rem(place + step, count)}, device_id_type=MESH
+        )
+    pl.semaphore_wait(barrier, 2 + count - 1)
+
+    def rows_of(k, s):
+        return pl.ds(k * chunk + s * part, part)
+
+    loads = []
+
+    def local(source, target, sem):
+        copy = pltpu.make_async_copy(source, target, sem)
+        copy.start()
+        return copy
+
+    dispatched = []
+    own_rows = None
+    for k in range(chips):
+        to = lax.rem(chip - k + chips, chips)
+        for c in range(2):
+            target = R.at[:, pl.ds(k * chunk + me * part + core * cap, cap)]
+            if k == 0:
+                if c == 0:
+                    own_rows = local(send_rows.at[place], target, own.at[0])
+                    dispatched.append(
+                        remote("fsdp", sibling, send_rows.at[sibling], target, z_send.at[0, 0], z_recv.at[0, 0])
+                    )
+                continue
+            peer = to * 2 + (core ^ c)
+            dispatched.append(
+                remote("fsdp", peer, send_rows.at[peer], target, z_send.at[k, c], z_recv.at[k, c])
+            )
+
+    def z_arrived(k):
+        if k == 0:
+            own_rows.wait()
+            dispatched[0].wait_recv()
+        else:
+            dispatched[2 * k - 1].wait_recv()
+            dispatched[2 * k].wait_recv()
+
+    sent = {}
+
+    def spread_out(a, k):
+        for side, peer in enumerate((one, two)):
+            for order in range(2):
+                j = (order + side) % 2
+                target = (U, R)[a].at[j, rows_of(k, me)]
+                source = up_rows.at[k, j] if a == 0 else target
+                sent[a, k, side, j] = remote(
+                    "seq", peer, source, target, s_send.at[a, k, side, j], s_recv.at[a, k, side, j]
+                )
+
+    def relay(a, k):
+        for side, (origin, peer) in enumerate(((one, two), (two, one))):
+            sent[a, k, side, side].wait_recv()
+            block = (U, R)[a].at[side, rows_of(k, origin)]
+            sent[a, k, 2, side] = remote(
+                "seq", peer, block, block, y_send.at[a, k, side], y_recv.at[a, k, side]
+            )
+
+    def all_arrived(a, k):
+        for side in range(2):
+            sent[a, k, side, 1 - side].wait_recv()
+        for side in range(2):
+            sent[a, k, 2, side].wait_recv()
+
+    def experts(k, j):
+        rows = pl.ds(k * chunk, chunk)
+        logits = times(R[j, rows, :], RT[...])
+        lane = lax.broadcasted_iota(jnp.int32, logits.shape, 1)
+        logits = jnp.where(lane < experts_all, logits, MASKED)
+        powers = jnp.exp(logits - jnp.max(logits, axis=1, keepdims=True))
+        picked = jnp.sum(jnp.where(lane == place * 2 + j, powers, 0.0), axis=1, keepdims=True)
+        gate = picked / jnp.sum(powers, axis=1, keepdims=True)
+        G[j, rows, :] = (U[j, rows, :].astype(jnp.float32) * gate).astype(G.dtype)
+
+        @pl.loop(0, W1.shape[2] // TILE)
+        def _(t):
+            cols = pl.ds(pl.multiple_of(t * TILE, TILE), TILE)
+            v = times(R[j, rows, :], W1[j, :, cols])
+            grad = times_transposed(G[j, rows, :], W2[j, cols, :])
+            square = v * v
+            t = jnp.tanh(ROOT * v * (1.0 + 0.044715 * square))
+            half = 0.5 * (1.0 + t)
+            A[j, rows, cols] = (v * half).astype(A.dtype)
+            slope = half + 0.5 * v * (1.0 - t * t) * (ROOT * (1.0 + 0.134145 * square))
+            I[j, rows, cols] = (grad * slope).astype(I.dtype)
+
+        @pl.loop(0, W1.shape[1] // TILE)
+        def _(t):
+            cols = pl.ds(pl.multiple_of(t * TILE, TILE), TILE)
+            PB[0, j, rows, cols] = times(A[j, rows, :], W2[j, :, cols]).astype(PB.dtype)
+            PB[1, j, rows, cols] = times_transposed(I[j, rows, :], W1[j, cols, :]).astype(PB.dtype)
+
+    summed = {}
+
+    def near_of(j):
+        return (one, two) if j == 0 else (two, one)
+
+    def collect_one(k, j):
+        near, rest = near_of(j)
+        for a in range(2):
+            for order, block in enumerate((both, near)):
+                summed[a, k, j, order] = remote(
+                    "seq", near, PB.at[a, j, rows_of(k, block)], first.at[a, j, k, order],
+                    c_send.at[a, j, k, order], c_recv.at[a, j, k, order],
+                )
+
+    def collect_two(k, j):
+        near, rest = near_of(j)
+        for a in range(2):
+            summed[a, k, j, 0].wait_recv()
+            first[a, j, k, 0] = (
+                first[a, j, k, 0].astype(jnp.float32) + PB[a, j, rows_of(k, rest), :].astype(jnp.float32)
+            ).astype(first.dtype)
+            summed[a, k, j, 2] = remote(
+                "seq", rest, first.at[a, j, k, 0], second.at[a, j, k], d_send.at[a, j, k], d_recv.at[a, j, k]
+            )
+
+    returns = {}
+
+    def collect_three(k, j):
+        for a in range(2):
+            summed[a, k, j, 1].wait_recv()
+            summed[a, k, j, 2].wait_recv()
+            first[a, j, k, 1] = (
+                first[a, j, k, 1].astype(jnp.float32)
+                + PB[a, j, rows_of(k, me), :].astype(jnp.float32)
+                + second[a, j, k].astype(jnp.float32)
+            ).astype(first.dtype)
+            to = lax.rem(chip + k, chips)
+            target = ret.at[a, place, j]
+            for c in range(2):
+                if k == 0:
+                    if c == 0:
+                        returns[a, k, j, 0] = local(
+                            first.at[a, j, k, 1, pl.ds(core * cap, cap)], target, own.at[1 + a * 2 + j]
+                        )
+                        returns[a, k, j, 1] = remote(
+                            "fsdp", sibling, first.at[a, j, k, 1, pl.ds((core ^ 1) * cap, cap)], target,
+                            r_send.at[a, j, k, 1], r_recv.at[a, j, k, 1],
+                        )
+                    continue
+                returns[a, k, j, c] = remote(
+                    "fsdp", to * 2 + (core ^ c), first.at[a, j, k, 1, pl.ds((core ^ c) * cap, cap)], target,
+                    r_send.at[a, j, k, c], r_recv.at[a, j, k, c],
+                )
+
+    staged = {}
+
+    def weight_grads(j, which):
+        left, right, out = ((R, I, dw_in), (A, G, dw_out))[which]
+        for m in range(left.shape[2] // GRAD):
+            slot = m % 2
+            lanes = slice(m * GRAD, (m + 1) * GRAD)
+            if slot in staged:
+                staged.pop(slot).wait()
+
+            @pl.loop(0, right.shape[2] // TILE)
+            def _(t):
+                cols = pl.ds(pl.multiple_of(t * TILE, TILE), TILE)
+                stage[slot, :, cols] = transposed_times(left[j, :, lanes], right[j, :, cols])
+
+            staged[slot] = local(stage.at[slot], out.at[j, lanes], store.at[slot])
+
+    mine = [
+        local(up_rows.at[k, j], U.at[j, rows_of(k, me)], own.at[5 + k * 2 + j])
+        for k in range(chips)
+        for j in range(2)
+    ]
+    spread_out(0, 0)
+    for j in range(2):
+        loads.append(local(w_in.at[j], W1.at[j], load.at[j]))
+        loads.append(local(w_out.at[j], W2.at[j], load.at[2 + j]))
+    loads.append(local(route, RT, load.at[4]))
+    z_arrived(0)
+    spread_out(1, 0)
+    spread_out(0, 1)
+    for copy in mine + loads:
+        copy.wait()
+    for k in range(chips):
+        relay(0, k)
+        relay(1, k)
+        if k + 1 < chips:
+            z_arrived(k + 1)
+            spread_out(1, k + 1)
+        if k + 2 < chips:
+            spread_out(0, k + 2)
+        all_arrived(0, k)
+        all_arrived(1, k)
+        experts(k, 0)
+        collect_one(k, 0)
+        if k:
+            collect_two(k - 1, 0)
+            collect_two(k - 1, 1)
+        experts(k, 1)
+        collect_one(k, 1)
+        if k:
+            collect_three(k - 1, 0)
+            collect_three(k - 1, 1)
+    last = chips - 1
+    weight_grads(0, 0)
+    collect_two(last, 0)
+    collect_two(last, 1)
+    weight_grads(0, 1)
+    weight_grads(1, 0)
+    collect_three(last, 0)
+    collect_three(last, 1)
+    weight_grads(1, 1)
+    for copy in staged.values():
+        copy.wait()
+    for copy in dispatched:
+        copy.wait_send()
+    for copy in sent.values():
+        copy.wait_send()
+    for copy in summed.values():
+        copy.wait_send()
+    for (a, k, j, c), copy in returns.items():
+        copy.wait()
+
+
+def moe(send_rows, up_rows, route, w_in, w_out, experts_all, number):
+    S, low, dma = jax.ShapeDtypeStruct, jnp.bfloat16, pltpu.SemaphoreType.DMA
+    owners, _, cap, width = send_rows.shape
+    chips = owners // 2
+    hidden_units = w_in.shape[2]
+    count = owners * cap * 4
+    part = 2 * cap
+
+    def vmem(*shape, dtype=low):
+        return pltpu.VMEM(shape, dtype)
+
+    return pl.pallas_call(
+        functools.partial(moe_kernel, chips, cap, experts_all),
+        out_shape=(
+            S((2, owners, 2, cap, width), low),
+            S(w_in.shape, jnp.float32),
+            S(w_out.shape, jnp.float32),
+        ),
+        in_specs=[ANY] * 5,
+        out_specs=(ANY,) * 3,
+        scratch_shapes=[
+            vmem(2, count, width),
+            vmem(2, count, width),
+            vmem(2, count, width),
+            vmem(2, count, hidden_units),
+            vmem(2, count, hidden_units),
+            vmem(2, 2, count, width),
+            vmem(2, 2, chips, 2, part, width),
+            vmem(2, 2, chips, part, width),
+            vmem(*w_in.shape),
+            vmem(*w_out.shape),
+            vmem(*route.shape),
+            vmem(2, GRAD, max(width, hidden_units), dtype=jnp.float32),
+            dma((5,)),
+            dma((5 + 2 * chips,)),
+            dma((chips, 2)),
+            dma((chips, 2)),
+            dma((2, chips, 2, 2)),
+            dma((2, chips, 2, 2)),
+            dma((2, chips, 2)),
+            dma((2, chips, 2)),
+            dma((2, 2, chips, 2)),
+            dma((2, 2, chips, 2)),
+            dma((2, 2, chips)),
+            dma((2, 2, chips)),
+            dma((2, 2, chips, 2)),
+            dma((2, 2, chips, 2)),
+            dma((2,)),
+        ],
+        compiler_params=pltpu.CompilerParams(
+            collective_id=number, has_side_effects=True, vmem_limit_bytes=58 * 2**20
+        ),
+        cost_estimate=pl.CostEstimate(
+            flops=12 * 2 * count * width * hidden_units, bytes_accessed=2**25, transcendentals=0
+        ),
+    )(send_rows, up_rows, route, w_in, w_out)
 
 
 def masked_scores(block_query, keys, start, length, scale):
@@ -395,7 +696,13 @@
     upstream_low = jnp.where(valid > 0, out_grad[0], 0).astype(low)
     upstream = upstream_low.astype(jnp.float32)
     up_rows = times(dispatch, upstream_low).astype(low)
-    up_all = spread(to_owners(up_rows, 0), 1)
+    up_all = to_owners(up_rows, 0)
+    fused = expert_local == 2 and 4 * owners * capacity <= 1024
+    if fused:
+        up_all = up_all.reshape(expert_local, owners // 2, 2 * capacity, width).transpose(1, 0, 2, 3)
+        up_all = jnp.roll(up_all, -(lax.axis_index("fsdp") // 2), axis=0)
+    else:
+        up_all = spread(up_all, 1)
 
     weight_qkv = columns_of(
         qkv_weight.reshape(rows_own, 3, seq_count, group_width)
@@ -444,36 +751,48 @@
         return jnp.sum(jnp.where(choose, jax.nn.softmax(logit_rows, axis=-1), 0.0), axis=-1)
 
     gate, gate_back = jax.vjp(gate_of, logits)
-    gate_rows = jnp.sum(jnp.where(hit, gate[None, :], 0.0), axis=1)
-    gates = lax.all_to_all(
-        gate_rows.reshape(owners, expert_local, capacity), "fsdp", split_axis=0, concat_axis=0, tiled=True
-    )
-    gates = lax.all_gather(gates, "seq", axis=0)
-    gates = gates.transpose(2, 0, 1, 3).reshape(expert_local, seq_count * owners * capacity, 1)
-
     sent = times(dispatch, normed_two).astype(low)
-    rows_all = spread(to_owners(sent, 5), 6)
-    count = seq_count * owners * capacity
-    rows_all = rows_all.reshape(expert_local, count, width)
-    up_all = up_all.reshape(expert_local, count, width)
-    grad_rows = (up_all.astype(jnp.float32) * gates).astype(low)
-
-    def per_expert(form, left, right):
-        return jnp.einsum(form, left, right, preferred_element_type=jnp.float32)
-
-    inner = per_expert("jrd,jdf->jrf", rows_all, expert_in)
-    active, active_back = jax.vjp(gelu_tanh, inner)
-    active = active.astype(low)
-    partial_out = per_expert("jrf,jfd->jrd", active, expert_out).astype(low)
-    grad_active = per_expert("jrd,jfd->jrf", grad_rows, expert_out)
-    grad_inner = active_back(grad_active)[0].astype(low)
-    partial_back = per_expert("jrf,jdf->jrd", grad_inner, expert_in).astype(low)
-    expert_out_grad = per_expert("jrf,jrd->jfd", active, grad_rows)
-    expert_in_grad = per_expert("jrd,jrf->jdf", rows_all, grad_inner)
-
-    shape = (expert_local, seq_count, owners * capacity, width)
-    returned = to_sources(collect(partial_out.reshape(shape), 7), 8)
-    grad_back = to_sources(collect(partial_back.reshape(shape), 9), 10)
+    if fused:
+        (returned, grad_back), expert_in_grad, expert_out_grad = moe(
+            sent.reshape(owners, expert_local, capacity, width),
+            up_all,
+            small,
+            expert_in,
+            expert_out,
+            experts_all,
+            5,
+        )
+        returned, grad_back = returned.reshape(slots, width), grad_back.reshape(slots, width)
+    else:
+        gate_rows = jnp.sum(jnp.where(hit, gate[None, :], 0.0), axis=1)
+        gates = lax.all_to_all(
+            gate_rows.reshape(owners, expert_local, capacity), "fsdp", split_axis=0, concat_axis=0, tiled=True
+        )
+        gates = lax.all_gather(gates, "seq", axis=0)
+        gates = gates.transpose(2, 0, 1, 3).reshape(expert_local, seq_count * owners * capacity, 1)
+
+        rows_all = spread(to_owners(sent, 5), 6)
+        count = seq_count * owners * capacity
+        rows_all = rows_all.reshape(expert_local, count, width)
+        up_all = up_all.reshape(expert_local, count, width)
+        grad_rows = (up_all.astype(jnp.float32) * gates).astype(low)
+
+        def per_expert(form, left, right):
+            return jnp.einsum(form, left, right, preferred_element_type=jnp.float32)
+
+        inner = per_expert("jrd,jdf->jrf", rows_all, expert_in)
+        active, active_back = jax.vjp(gelu_tanh, inner)
+        active = active.astype(low)
+        partial_out = per_expert("jrf,jfd->jrd", active, expert_out).astype(low)
+        grad_active = per_expert("jrd,jfd->jrf", grad_rows, expert_out)
+        grad_inner = active_back(grad_active)[0].astype(low)
+        partial_back = per_expert("jrf,jdf->jrd", grad_inner, expert_in).astype(low)
+        expert_out_grad = per_expert("jrf,jrd->jfd", active, grad_rows)
+        expert_in_grad = per_expert("jrd,jrf->jdf", rows_all, grad_inner)
+
+        shape = (expert_local, seq_count, owners * capacity, width)
+        returned = to_sources(collect(partial_out.reshape(shape), 7), 8)
+        grad_back = to_sources(collect(partial_back.reshape(shape), 9), 10)
 
     back_rows = transposed_times(dispatch, returned)
     output = valid * (middle + gate[:, None] * back_rows)

time: 732 us -> 595 us (0.81)
  matrix products: 96.3 us -> 35.9 us
  Pallas kernels: 379 us -> 340 us
  waiting for transfers between devices: 128 us -> 97.1 us
  local copies, waits for them, and re-layouts: 18.7 us -> 38.8 us
  starting transfers between devices: 9.75 us -> 0.08 us
  blocking collectives: 52.3 us -> 44.5 us
    pallas_call x15 -> x8, Pallas kernels: 379 us -> 166 us  [call(): pl.pallas_call(kernel, out_shape=outputs, in_specs=[ANY] * len(inputs), o...]
    pallas_call x0 -> x1, Pallas kernels: none -> 174 us  [moe(): pl.pallas_call(functools.partial(moe_kernel, chips, cap, experts_all), ou...]
    dot_general x6 -> x0, matrix products: 60.1 us -> none  [per_expert(): return jnp.einsum(form, left, right, preferred_element_type=jnp.float32)]
    unnamed x3, waiting for transfers between devices: 123 us -> 97.1 us
    unnamed x94 -> x74, local copies, waits for them, and re-layouts: 8.03 us -> 24.7 us
    all_to_all x1 -> x0, starting transfers between devices: 9.67 us -> none  [shards(): lax.all_to_all(gate_rows.reshape(owners, expert_local, capacity), 'fsdp',...]
    all_gather x1 -> x0, blocking collectives: 7.81 us -> none  [shards(): gates = lax.all_gather(gates, 'seq', axis=0)]
  transfers between devices with their start and end apart: 3 -> 2, of which waited for: 2 -> 1; matrix products, arithmetic and copies ran while one was open for 6% -> 6% of each run, Pallas kernels for 17% -> 21%
where the time goes in v3:
time: 595 us; the launch traced here: 592 us
  Pallas kernels  340 us (57%)
  waiting for transfers between devices  97.1 us (16%)
  blocking collectives  44.5 us (7%)
  local copies, waits for them, and re-layouts  38.8 us (7%)
  matrix products  35.9 us (6%)
  other arithmetic  20.3 us (3%)
  between operations  15.7 us (3%)
    pallas_call x1, Pallas kernels, moe(): pl.pallas_call(functools.partial(moe_kernel, chips, cap, experts_all), ou...  174 us
    pallas_call x8, Pallas kernels, call(): pl.pallas_call(kernel, out_shape=outputs, in_specs=[ANY] * len(inputs), o...  166 us
    unnamed x3, waiting for transfers between devices  97.1 us
    all_gather x1, blocking collectives, shards(): small = lax.all_gather(small, ('seq', 'fsdp'), axis=0, tiled=True)  44.5 us
    unnamed x74, local copies, waits for them, and re-layouts  24.7 us
  transfers between devices with their start and end apart: 2, of which 1 were waited for; matrix products, arithmetic and copies ran while one was open for 6% of the time, Pallas kernels for 21%

profile of v3, /device:TPU:0, one launch (start us, length us, event | category | flops | bytes accessed | tf_op | source)
XLA Modules:
  0.0 592.0 jit_solution(4840401417456510788)
XLA Ops:
  7.2 0.7 all-gather.2.cloned.1.call-update
  8.7 0.9 convert_reduce_fusion.4
  9.6 0.7 multiply_add_fusion.1
  10.3 0.8 copy.66
  11.1 0.8 copy.67
  11.8 0.8 copy.65
  12.6 1.1 reshape.425
  14.1 44.5 %all_gather.6.route = bf16[1024,128]{1,0:T(8,128)(2,1)S(1)} all-gather(bf16[32,128]{1,0:T(8,128)(2,1)S(1)} %fusion.48), channel_id=1, replica_groups=mesh['seq'=4,'fsdp'=8] {'seq','fsdp'}, dimensions={0}, use_global_device_ids=true | all-gather | bytes 270336 | tf_op jit(solution)/shard_map/all_gather | solution.py:654
  59.1 1.7 convolution_convert_fusion.3
  60.8 20.6 %shard_map.191 = bf16[2,8,32,1024]{3,2,1,0:T(8,128)(2,1)S(1)} custom-call(bf16[8,2,32,1024]{3,2,1,0:T(8,128)(2,1)S(1)} %bitcast.152), custom_call_target="tpu_custom_call" | custom-call | tf_op jit(solution)/shard_map/pallas_call | solution.py:61
  81.5 1.0 copy-done.1
  82.4 28.3 %shard_map.189 = bf16[4,8,32,768]{3,2,1,0:T(8,128)(2,1)S(1)} custom-call(bf16[4,32,768]{2,1,0:T(8,128)(2,1)S(1)} %reshape.426.source), custom_call_target="tpu_custom_call" | custom-call | tf_op jit(solution)/shard_map/pallas_call | solution.py:61
  110.7 21.2 %shard_map.188 = bf16[1,4,256,1024]{3,2,1,0:T(8,128)(2,1)S(1)} custom-call(bf16[1,256,1024]{2,1,0:T(8,128)(2,1)S(1)} %copy-done), custom_call_target="tpu_custom_call" | custom-call | tf_op jit(solution)/shard_map/pallas_call | solution.py:61
  133.0 1.9 convolution_convert_fusion.2
  135.4 0.9 fusion.4
  136.4 0.9 exponential_reduce_fusion.1
  137.4 1.7 fusion
  139.1 2.4 exponential_reduce_fusion
  141.6 1.3 fusion.17
  142.9 2.3 fusion.16
  145.4 0.9 copy-done.25
  146.2 1.2 reshape_reshape.6
  147.4 1.3 copy.70.refs_0_
  148.7 8.4 %shard_map.190 = bf16[4,256,256]{2,1,0:T(8,128)(2,1)S(1)} custom-call(bf16[4,256,256]{2,1,0:T(8,128)(2,1)S(1)} %copy.70.refs_0_), custom_call_target="tpu_custom_call" | custom-call | tf_op jit(solution)/shard_map/pallas_call | solution.py:61
  157.1 0.8 copy-done.2
  157.9 1.2 copy.71
  159.1 1.3 copy_bitcast_fusion
  160.5 1.5 fusion.24.up_rows
  162.1 1.8 fusion.3
  164.0 2.4 multiply_reduce_fusion.5
  166.8 1.4 convolution_convert_fusion.4
  168.3 173.6 %shard_map.192 = (bf16[2,8,2,32,1024]{4,3,2,1,0:T(8,128)(2,1)}, f32[2,1024,1024]{2,1,0:T(8,128)}, f32[2,1024,1024]{2,1,0:T(8,128)}) custom-call(bf16[8,2,32,1024]{3,2,1,0:T(8,128)(2,1)} %bitcast.177, bf16[4,2,64,1024]{3,2,1,0:T(8,128)(2,1)} %fusion.24.up_rows, bf16[1024,128]{1,0:T(8,128)(2,1)} %copy-done.11, bf16[2,1024,1024]{2,1,0:T(8,128)(2,1)} %w_in.1, ...), custom_call_target="tpu_custom_call" | custom-call | flops 25769803776 | bytes 33554432 | tf_op jit(solution)/shard_map/pallas_call | solution.py:569
  341.9 1.8 fusion.62
  344.9 0.7 multiply_reduce_fusion.3
  345.6 1.6 convert_bitcast_fusion
  347.3 20.7 %shard_map.193 = bf16[1,4,256,1024]{3,2,1,0:T(8,128)(2,1)S(1)} custom-call(bf16[1,256,1024]{2,1,0:T(8,128)(2,1)S(1)} %get-tuple-element.91.source), custom_call_target="tpu_custom_call" | custom-call | tf_op jit(solution)/shard_map/pallas_call | solution.py:61
  368.0 1.8 convolution_convert_fusion.6
  369.9 1.2 convolution_bitcast_fusion.1
  371.1 1.5 multiply_reduce_fusion.1
  372.6 1.2 multiply_convert_fusion.1
  374.3 0.8 fusion.13
  375.3 3.2 multiply_reduce_fusion
  378.5 2.5 fusion.11
  381.0 2.5 multiply_convert_fusion
  383.5 1.4 fusion.15
  384.9 0.8 fusion.10
  386.3 1.8 convolution_convert_fusion
  388.2 3.0 convolution_convert_fusion.1
  391.2 19.6 %shard_map.194 = bf16[1,256,1024]{2,1,0:T(8,128)(2,1)S(1)} custom-call(bf16[1,4,256,1024]{3,2,1,0:T(8,128)(2,1)S(1)} %bitcast.147), custom_call_target="tpu_custom_call" | custom-call | tf_op jit(solution)/shard_map/pallas_call | solution.py:61
  411.4 1.0 copy.86
  412.4 1.9 pad.21.clone
  414.3 1.9 convolution_convert_fusion.5
  416.2 38.7 %shard_map.195 = (bf16[8,4,32,768]{3,2,1,0:T(8,128)(2,1)S(1)}, bf16[8,32,1024]{2,1,0:T(8,128)(2,1)S(1)}) custom-call(bf16[4,8,32,768]{3,2,1,0:T(8,128)(2,1)S(1)} %bitcast.151, bf16[8,32,1024]{2,1,0:T(8,128)(2,1)S(1)} %bitcast.153), custom_call_target="tpu_custom_call" | custom-call | tf_op jit(solution)/shard_map/pallas_call | solution.py:61
  455.1 8.5 %shard_map.196 = f32[4,32,768]{2,1,0:T(8,128)S(1)} custom-call(f32[4,32,768]{2,1,0:T(8,128)S(1)} %convert_reduce_fusion.refs_0_), custom_call_target="tpu_custom_call" | custom-call | tf_op jit(solution)/shard_map/pallas_call | solution.py:61
  464.1 0.9 reshape.441
  465.0 0.7 convert_reduce_fusion.1
  465.8 2.5 fusion.21
  468.3 96.4 %reduce-scatter.4.cloned.1.call-done = f32[32,128]{1,0:T(8,128)} async-done(((f32[1024,128]{1,0:T(8,128)}), f32[32,128]{1,0:T(8,128)}) %reduce-scatter.4.cloned.1.call-update) | async-done | bytes 16400
  564.7 1.4 copy.85
  566.1 0.9 fusion.66
  566.9 0.6 copy.84
  567.5 0.6 copy.83
  568.1 8.4 %copy.94 = f32[2,1024,1024]{2,1,0:T(8,128)} copy(f32[2,1024,1024]{2,1,0:T(8,128)} %get-tuple-element.141) | data formatting | bytes 16777216
  576.5 8.4 %copy.95 = f32[2,1024,1024]{2,1,0:T(8,128)} copy(f32[2,1024,1024]{2,1,0:T(8,128)} %get-tuple-element.142) | data formatting | bytes 16777216
  (108 shorter events, 7.1 us)
Async XLA Ops:
  7.2 103.6 %copy-start = (bf16[1,256,1024]{2,1,0:T(8,128)(2,1)S(1)}, bf16[1,256,1024]{2,1,0:T(8,128)(2,1)}, u32[]{:S(2)}) copy-start(bf16[1,256,1024]{2,1,0:T(8,128)(2,1)} %source.1) | copy-start | bytes 1572868
  7.2 156.8 %all-gather.2.cloned.1.call-start = ((), (), s32[]{:S(2)}) async-start(), calls=%async_computation.1 | async-start | bytes 2162688 | tf_op jit(solution)/shard_map/all_gather | solution.py:655
  7.9 556.8 %reduce-scatter.4.cloned.1.call-start = ((), (), s32[]{:S(2)}) async-start(), calls=%async_computation.2 | async-start | bytes 540672
  58.6 107.9 %copy-start.11 = (bf16[1024,128]{1,0:T(8,128)(2,1)}, bf16[1024,128]{1,0:T(8,128)(2,1)S(1)}, u32[]{:S(2)}) copy-start(bf16[1024,128]{1,0:T(8,128)(2,1)S(1)} %all_gather.6.route) | copy-start | bytes 786436
  59.1 82.5 %copy-start.13 = (pred[512,512]{0,1:T(8,128)(4,1)}, pred[512,512]{0,1:T(8,128)(4,1)S(1)}, u32[]{:S(2)}) copy-start(pred[512,512]{0,1:T(8,128)(4,1)S(1)} %fusion.25) | copy-start | bytes 786436
  81.4 1.0 copy-start.1
  110.7 22.3 %copy-start.3 = (bf16[4,8,32,768]{3,2,1,0:T(8,128)(2,1)}, bf16[4,8,32,768]{3,2,1,0:T(8,128)(2,1)S(1)}, u32[]{:S(2)}) copy-start(bf16[4,8,32,768]{3,2,1,0:T(8,128)(2,1)S(1)} %shard_map.189) | copy-start | bytes 4718596
  135.0 2.3 copy-start.19
  135.0 2.3 copy-start.21
  135.0 2.4 copy-start.17
  135.0 6.6 %copy-start.28 = (bf16[512,256]{0,1:T(8,128)(2,1)}, bf16[512,256]{0,1:T(8,128)(2,1)S(1)}, u32[]{:S(2)}) copy-start(bf16[512,256]{0,1:T(8,128)(2,1)S(1)} %get-tuple-element.98) | copy-start | bytes 786436
  135.4 7.5 %copy-start.9 = (pred[512,1024]{1,0:T(8,128)(4,1)}, pred[512,1024]{1,0:T(8,128)(4,1)S(1)}, u32[]{:S(2)}) copy-start(pred[512,1024]{1,0:T(8,128)(4,1)S(1)} %fusion.6) | copy-start | bytes 1572868
  136.3 5.3 copy-start.7
  137.4 1.7 copy-start.15
  137.4 5.5 copy-start.26
  139.1 3.8 copy-start.6
  145.3 0.9 copy-start.25
  157.1 0.8 copy-start.2
  341.9 1.8 copy-start.23
  341.9 2.4 copy-start.30
  341.9 2.6 copy-start.12
  347.3 22.6 %copy-start.8 = (f32[4,512,512]{1,2,0:T(8,128)S(1)}, f32[4,512,512]{1,2,0:T(8,128)}, u32[]{:S(2)}) copy-start(f32[4,512,512]{1,2,0:T(8,128)} %copy-done.7) | copy-start | bytes 12582916
  347.3 22.6 %copy-start.14 = (pred[512,512]{0,1:T(8,128)(4,1)S(1)}, pred[512,512]{0,1:T(8,128)(4,1)}, u32[]{:S(2)}) copy-start(pred[512,512]{0,1:T(8,128)(4,1)} %copy-done.13) | copy-start | bytes 786436
  369.8 1.3 copy-start.29
  371.1 4.0 slice-start
  372.6 1.3 copy-start.20
  372.6 1.8 copy-start.22
  372.6 2.5 slice-start.1
  373.8 1.3 copy-start.10
  373.9 1.5 copy-start.27
  380.9 2.6 copy-start.16
  383.5 1.4 copy-start.18
  384.9 1.4 copy-start.4
  386.3 1.8 copy-start.24
  414.3 1.9 copy-start.5
Sparse Core Ops, SparseCore 0:
  11.0 70.2 all-gather.1
  414.4 150.2 reduce-scatter.3
